TPU v7x, 512 devices: a whole 4x8x8 slice. The times are simulated.
512 devices in a mesh: band: 8 (over z), grid: 64 (over y, x, core).
Axes of the slice: x: 4, y: 8, z: 8, core: 2. Of those that a mesh axis runs over, the one named last changes fastest.
Arguments:
- psi_g: float32 [2, 16, 3072, 128], P(None, 'band', 'grid'), may hold values from -6 to 6
- col_index: int32 [3072], P('grid'), may hold values from 0 to 16383, as said below
- v_local: float32 [128, 128, 128], P('grid'), may hold values from -4 to 4
- proj_values: float32 [16384, 18, 128], P('grid'), may hold values from -0.15625 to 0.15625
- pair_atom: int32 [16384], P('grid'), may hold values from 0 to 512, as said below
- pair_row: int32 [16384], P('grid'), may hold values from 0 to 16383, as said below
- d_matrices: float32 [512, 18, 18], P('grid'), may hold values from -1.5 to 1.5
- occupations: float32 [16], P('band'), may hold values from 0.2 to 2
Outputs:
- h_psi: float32 [2, 16, 3072, 128], P(None, 'band', 'grid')
- density: float32 [128, 128, 128], P('grid')
Inputs may be any that keep to these rules, and one draw needn't show every extreme that they name: `col_index`: distinct positions; the set is the 3072 positions of smallest fy^2 + fz^2, ties broken by the seed, dealt to the devices in a random order. `pair_atom`: an atom, or 512 for an empty slot. On each grid device the live slots come first; their number is an eighth, a quarter or all of its 256 slots, and some device has all slots live. The live slots of one atom lie on at most three devices of grid that follow one another cyclically (the last device is followed by the first). `pair_row`: the row lies in the planes of the device that holds the slot: device i of grid holds x from i * 2 to (i + 1) * 2 - 1. Rows may repeat.
All inputs are finite; a program needn't handle non-finite values.
Results may differ from a plain program's by a relative error of at most 0.0001.
Values sent between devices are 32-bit elements; how exact they have to be, the bound alone decides.
A program may use at most 64 MiB of HBM per device.

v0:
```python
import jax
import jax.numpy as jnp
from jax import lax
from jax.sharding import PartitionSpec as P

HIGH = lax.Precision.HIGHEST
KINETIC = 0.0005


def dft_tables(extent):
    positions = jnp.arange(extent, dtype=jnp.int32)
    phase = positions[:, None] * positions[None, :] % extent
    angle = phase.astype(jnp.float32) * (2.0 * jnp.pi / extent)
    scale_factor = 1.0 / jnp.sqrt(jnp.float32(extent))
    return (jnp.cos(angle) * scale_factor, jnp.sin(angle) * scale_factor)


def column_tables(col_all, extent):
    positions = jnp.arange(extent, dtype=jnp.int32)
    first_pos = col_all // extent
    second_pos = col_all % extent
    phase = first_pos[:, None] * positions[None, :] % extent
    angle = phase.astype(jnp.float32) * (2.0 * jnp.pi / extent)
    scale_factor = 1.0 / jnp.sqrt(jnp.float32(extent))
    picker = (second_pos[:, None] == positions[None, :]).astype(jnp.float32)
    return (jnp.cos(angle) * scale_factor, jnp.sin(angle) * scale_factor, picker)


def last_axis(real_part, imag_part, cosine, sine_table, direction):
    real_cos = jnp.matmul(real_part, cosine, precision=HIGH)
    real_sin = jnp.matmul(real_part, sine_table, precision=HIGH)
    imag_cos = jnp.matmul(imag_part, cosine, precision=HIGH)
    imag_sin = jnp.matmul(imag_part, sine_table, precision=HIGH)
    return (real_cos - direction * imag_sin, imag_cos + direction * real_sin)


def signed_freq(positions, extent):
    return jnp.where(positions >= extent // 2, positions - extent, positions)


def per_device(
    psi_g, col_index, v_local, proj_values, pair_atom, pair_row, d_matrices, occupations
):
    grid_count = lax.axis_size("grid")
    extent = psi_g.shape[3]
    band_count = psi_g.shape[1]
    planes = extent // grid_count
    row_count = planes * extent
    cosine, sine_table = dft_tables(extent)
    col_real, col_imag = last_axis(psi_g[0], psi_g[1], cosine, sine_table, 1.0)
    columns = jnp.stack([col_real, col_imag])
    col_all = lax.all_gather(col_index, "grid", axis=0, tiled=True)
    col_cos, col_sin, picker = column_tables(col_all, extent)
    pieces = [
        lax.all_to_all(
            columns[:, member : member + 1], "grid", split_axis=3, concat_axis=2, tiled=True
        )
        for member in range(band_count)
    ]
    spread = jnp.concatenate(pieces, axis=1)
    spread_real = spread[0][:, :, :, None]
    spread_imag = spread[1][:, :, :, None]
    phase_cos = col_cos[None, :, None, :]
    phase_sin = col_sin[None, :, None, :]
    rows_real = spread_real * phase_cos - spread_imag * phase_sin
    rows_imag = spread_real * phase_sin + spread_imag * phase_cos
    real_part = jnp.einsum("bcxy,cz->bxyz", rows_real, picker, precision=HIGH)
    imag_part = jnp.einsum("bcxy,cz->bxyz", rows_imag, picker, precision=HIGH)
    real_part, imag_part = last_axis(real_part, imag_part, cosine, sine_table, 1.0)
    weights = occupations[:, None, None, None]
    density_part = jnp.sum(weights * (real_part * real_part + imag_part * imag_part), axis=0)
    density = lax.psum(density_part, "band")
    field = jnp.stack([real_part, imag_part]).reshape(2, band_count, row_count, extent)
    local_row = pair_row - lax.axis_index("grid") * row_count
    row_pick = (local_row[:, None] == jnp.arange(row_count, dtype=jnp.int32)[None, :]).astype(
        jnp.float32
    )
    tiles = jnp.einsum("pr,cbrz->cbpz", row_pick, field, precision=HIGH)
    pair_coeff = jnp.einsum("piz,cbpz->picb", proj_values, tiles, precision=HIGH)
    slot_count = proj_values.shape[0]
    proj_count = proj_values.shape[1]
    width_cols = proj_count * 2 * band_count
    atom_total = d_matrices.shape[0] * grid_count
    onehot = (pair_atom[None, :] == jnp.arange(atom_total, dtype=jnp.int32)[:, None]).astype(
        jnp.float32
    )
    partial_value = jnp.dot(onehot, pair_coeff.reshape(slot_count, width_cols), precision=HIGH)
    owned = lax.psum_scatter(partial_value, "grid", scatter_dimension=0, tiled=True)
    mine = jnp.einsum(
        "aij,ajk->aik",
        d_matrices,
        owned.reshape(d_matrices.shape[0], proj_count, 2 * band_count),
        precision=HIGH,
    )
    applied = lax.all_gather(mine, "grid", axis=0, tiled=True)
    per_slot = jnp.dot(onehot.T, applied.reshape(atom_total, width_cols), precision=HIGH)
    per_slot = per_slot.reshape(slot_count, proj_count, 2, band_count)
    added = jnp.einsum("piz,picb->cbpz", proj_values, per_slot, precision=HIGH)
    projected = jnp.einsum("pr,cbpz->cbrz", row_pick, added, precision=HIGH)
    h_rows = v_local.reshape(1, 1, row_count, extent) * field + projected
    h_block = h_rows.reshape(2, band_count, planes, extent, extent)
    real_part, imag_part = last_axis(h_block[0], h_block[1], cosine, sine_table, -1.0)
    taken_real = jnp.einsum("bxyz,cz->bcxy", real_part, picker, precision=HIGH)
    taken_imag = jnp.einsum("bxyz,cz->bcxy", imag_part, picker, precision=HIGH)
    back_cos = col_cos[None, :, None, :]
    back_sin = col_sin[None, :, None, :]
    picked_real = jnp.sum(taken_real * back_cos + taken_imag * back_sin, axis=3)
    picked_imag = jnp.sum(taken_imag * back_cos - taken_real * back_sin, axis=3)
    picked = jnp.stack([picked_real, picked_imag])
    returned = [
        lax.all_to_all(
            picked[:, member : member + 1], "grid", split_axis=2, concat_axis=3, tiled=True
        )
        for member in range(band_count)
    ]
    gathered = jnp.concatenate(returned, axis=1)
    back_real, back_imag = last_axis(gathered[0], gathered[1], cosine, sine_table, -1.0)
    first_freq = signed_freq(col_index // extent, extent)
    second_freq = signed_freq(col_index % extent, extent)
    third_freq = signed_freq(jnp.arange(extent, dtype=jnp.int32), extent)
    square = (first_freq * first_freq + second_freq * second_freq)[:, None] + (
        third_freq * third_freq
    )[None, :]
    kinetic = KINETIC * square.astype(jnp.float32)
    h_psi = jnp.stack([back_real, back_imag]) + kinetic[None, None] * psi_g
    return (h_psi, density)


def solution(mesh):
    placed = (
        P(None, "band", "grid", None),
        P("grid"),
        P("grid", None, None),
        P("grid", None, None),
        P("grid"),
        P("grid"),
        P("grid", None, None),
        P("band"),
    )
    return jax.shard_map(
        per_device,
        mesh=mesh,
        in_specs=placed,
        out_specs=(P(None, "band", "grid", None), P("grid", None, None)),
        check_vma=False,
    )
```

profile of v0, /device:TPU:1, one launch (start us, length us, event | category | flops | bytes accessed | tf_op | source)
XLA Modules:
  0.0 709.7 jit_solution(14868984244481868742)
XLA Ops:
  8.0 1.4 fusion.89
  9.4 1.3 fusion.91
  10.7 1.3 fusion.46
  12.0 1.3 fusion.47
  13.4 0.6 broadcast.298
  14.0 1.1 reduce.2
  15.1 0.8 reshape.137
  15.9 11.6 %all-to-all-start = ((f32[64,1,192]{2,1,0:T(1,128)}), f32[64,1,192]{2,1,0:T(1,128)S(1)}, u32[]{:S(2)}, u32[]{:S(2)}) async-start(f32[64,1,192]{2,1,0:T(1,128)} %reshape.137), calls=%async_computation | async-start | bytes 131072 | tf_op jit(solution)/shard_map/all_to_all | solution.py:55
  27.5 1.4 fusion.205
  29.5 0.9 dynamic-update-slice
  30.4 245.9 %all-reduce = s32[3072]{0:T(1024)S(1)} all-reduce(s32[3072]{0:T(1024)S(1)} %dynamic-update-slice), channel_id=1, replica_groups=mesh['band'=8,'grid'=64] {'grid'}, use_global_device_ids=true, to_apply=%add | all-reduce | flops 3072 | bytes 24576
  276.3 7.2 %cosine_multiply_fusion = (f32[3072,128]{0,1:T(8,128)}, f32[3072,128]{0,1:T(8,128)}) fusion(s32[3072]{0:T(1024)S(1)} %get-tuple-element.13), kind=kLoop, calls=%fused_computation.29 | loop fusion | flops 6291456 | bytes 3158016 | tf_op jit(solution)/shard_map/mul | solution.py:26
  283.7 1.1 reduce.4
  284.8 0.8 reshape.139
  285.6 10.6 %all-to-all-start.1 = ((f32[64,1,192]{2,1,0:T(1,128)}), f32[64,1,192]{2,1,0:T(1,128)S(1)}, u32[]{:S(2)}, u32[]{:S(2)}) async-start(f32[64,1,192]{2,1,0:T(1,128)} %reshape.139), calls=%async_computation.1 | async-start | bytes 131072 | tf_op jit(solution)/shard_map/all_to_all | solution.py:55
  296.5 0.8 reduce.3
  297.8 8.5 %all-to-all-done.1 = f32[64,1,192]{2,1,0:T(1,128)S(1)} async-done(((f32[64,1,192]{2,1,0:T(1,128)}), f32[64,1,192]{2,1,0:T(1,128)S(1)}, u32[]{:S(2)}, u32[]{:S(2)}) %all-to-all-start.1) | async-done | bytes 49184 | tf_op jit(solution)/shard_map/all_to_all | solution.py:55
  306.3 0.8 reduce.5
  307.6 5.7 fusion
  313.4 3.8 fusion.4
  317.2 0.6 fusion.79
  317.8 0.6 fusion.77
  318.4 0.6 convolution_subtract_fusion
  319.1 1.3 multiply_reduce_fusion
  320.7 0.5 convolution_bitcast_fusion.1
  321.2 1.0 copy.72
  322.2 7.4 %fusion.33 = f32[256,18,2,2]{1,3,2,0:T(2,128)S(1)} fusion(f32[2,2,256,128]{3,1,0,2:T(2,128)} %copy.72, f32[256,18,128,1]{2,0,1,3:T(8,128)S(1)} %bitcast.172), kind=kOutput, calls=%fused_computation.37 | convolution fusion | flops 28311552 | bytes 2957312 | tf_op jit(solution)/shard_map/piz,cbpz->picb/dot_general | solution.py:79
  329.9 1.7 fusion.54
  331.7 1.2 fusion.116
  332.9 1.6 copy.63
  335.2 180.8 %all-reduce.7.cloned.1.call-done = f32[512,72]{1,0:T(8,128)} async-done(((f32[512,72]{1,0:T(8,128)}), f32[512,72]{1,0:T(8,128)}) %all-reduce.7.cloned.1.call-update) | async-done | bytes 147472
  516.0 0.7 constant_dynamic-slice_fusion
  517.1 48.1 %all_gather.7 = f32[512,18,4]{1,2,0:T(4,128)S(1)} all-gather(f32[8,18,4]{1,2,0:T(4,128)S(1)} %convolution_bitcast_fusion.2), channel_id=1, replica_groups=mesh['band'=8,'grid'=64] {'grid'}, dimensions={0}, use_global_device_ids=true | all-gather | bytes 149760 | tf_op jit(solution)/shard_map/all_gather | solution.py:95
  565.7 1.7 fusion.55
  567.4 1.3 copy.80
  568.7 4.5 fusion.36
  573.3 0.7 fusion.39
  574.1 0.6 fusion.73
  574.9 0.6 fusion.75
  575.5 0.6 fusion.40
  576.1 0.6 fusion.41
  576.8 3.9 fusion.29
  580.7 5.9 add_reduce_fusion
  586.6 3.4 copy.87
  590.0 5.7 reshape.143
  595.8 7.0 all-to-all-start.2
  602.8 3.4 copy.90
  606.2 5.7 reshape.141
  611.9 1.0 all-to-all-done.2
  612.8 9.3 %all-to-all-start.3 = ((f32[64,1,192]{2,1,0:T(1,128)}), f32[64,1,192]{2,1,0:T(1,128)S(1)}, u32[]{:S(2)}, u32[]{:S(2)}) async-start(f32[64,1,192]{2,1,0:T(1,128)} %reshape.141), calls=%async_computation.3 | async-start | bytes 131072 | tf_op jit(solution)/shard_map/all_to_all | solution.py:111
  622.3 0.4 all-reduce.5.cloned.1.call-update
  622.8 0.8 reduce.7
  623.6 6.4 reshape.144
  630.1 5.0 copy.106
  635.2 0.8 reduce.6
  636.1 6.4 reshape.142
  642.5 5.0 copy.107
  647.8 0.5 fusion.87
  648.2 0.4 fusion.85
  648.7 0.5 fusion.45
  649.1 0.5 fusion.43
  649.6 0.7 maximum_add_fusion
  650.3 50.0 %all-reduce.5.cloned.1.call-done = f32[2,128,128]{2,1,0:T(8,128)} async-done(((f32[2,128,128]{2,1,0:T(8,128)}), f32[2,128,128]{2,1,0:T(8,128)}) %all-reduce.5.cloned.1.call-update) | async-done | bytes 131088 | tf_op jit(solution)/shard_map/psum | solution.py:72
  700.3 1.6 copy.128
  (80 shorter events, 3.8 us)
Async XLA Ops:
  8.0 314.2 %copy-start = (f32[256,18,128]{2,0,1:T(8,128)S(1)}, f32[256,18,128]{2,0,1:T(8,128)}, u32[]{:S(2)}) copy-start(f32[256,18,128]{2,0,1:T(8,128)} %param.11) | copy-start | bytes 7077892
  10.7 272.9 %copy-start.16 = (s32[256]{0:T(256)S(1)}, s32[256]{0:T(256)}, u32[]{:S(2)}) copy-start(s32[256]{0:T(256)} %param.13) | copy-start | bytes 3076
  15.9 269.7 %all-to-all-start = ((f32[64,1,192]{2,1,0:T(1,128)}), f32[64,1,192]{2,1,0:T(1,128)S(1)}, u32[]{:S(2)}, u32[]{:S(2)}) async-start(f32[64,1,192]{2,1,0:T(1,128)} %reshape.137), calls=%async_computation | async-start | bytes 131072 | tf_op jit(solution)/shard_map/all_to_all | solution.py:55
  276.3 37.1 %copy-start.11 = (s32[3072]{0:T(1024)}, s32[3072]{0:T(1024)S(1)}, u32[]{:S(2)}) copy-start(s32[3072]{0:T(1024)S(1)} %get-tuple-element.12) | copy-start | bytes 36868
  283.6 37.1 %copy-start.14 = (s32[256]{0:T(256)}, s32[256]{0:T(256)S(1)}, u32[]{:S(2)}) copy-start(s32[256]{0:T(256)S(1)} %broadcast_subtract_fusion) | copy-start | bytes 3076
  285.6 20.7 %all-to-all-start.1 = ((f32[64,1,192]{2,1,0:T(1,128)}), f32[64,1,192]{2,1,0:T(1,128)S(1)}, u32[]{:S(2)}, u32[]{:S(2)}) async-start(f32[64,1,192]{2,1,0:T(1,128)} %reshape.139), calls=%async_computation.1 | async-start | bytes 131072 | tf_op jit(solution)/shard_map/all_to_all | solution.py:55
  296.2 219.8 %all-reduce.7.cloned.1.call-start = ((), (), s32[]{:S(2)}) async-start(), calls=%async_computation.5 | async-start | bytes 524288
  307.6 5.8 copy-start.1
  307.6 5.8 copy-start.3
  313.4 5.7 copy-start.17
  320.5 9.0 %copy-start.5 = (f32[1,2,256,128]{2,3,1,0:T(8,128)}, f32[1,2,256,128]{2,3,1,0:T(8,128)S(1)}, u32[]{:S(2)}) copy-start(f32[1,2,256,128]{2,3,1,0:T(8,128)S(1)} %copy.71) | copy-start | bytes 786436
  320.7 8.9 %copy-start.7 = (f32[1,2,256,128]{2,3,1,0:T(8,128)}, f32[1,2,256,128]{2,3,1,0:T(8,128)S(1)}, u32[]{:S(2)}) copy-start(f32[1,2,256,128]{2,3,1,0:T(8,128)S(1)} %copy.70) | copy-start | bytes 786436
  322.2 194.7 %copy-start.10 = (f32[8,18,18]{2,0,1:T(8,128)S(1)}, f32[8,18,18]{2,0,1:T(8,128)}, u32[]{:S(2)}) copy-start(f32[8,18,18]{2,0,1:T(8,128)} %param.14) | copy-start | bytes 31108
  567.4 5.9 copy-start.6
  567.4 5.9 copy-start.8
  567.4 5.9 copy-start.9
  567.4 5.9 copy-start.15
  573.9 2.8 copy-start.12
  576.8 3.9 copy-start.2
  576.8 3.9 copy-start.4
  595.8 17.1 %all-to-all-start.2 = ((f32[64,1,192]{2,1,0:T(1,128)}), f32[64,1,192]{2,1,0:T(1,128)S(1)}, u32[]{:S(2)}, u32[]{:S(2)}) async-start(f32[64,1,192]{2,1,0:T(1,128)} %reshape.143), calls=%async_computation.2 | async-start | bytes 131072 | tf_op jit(solution)/shard_map/all_to_all | solution.py:111
  606.1 16.1 %copy-start.18 = (s32[48]{0:T(128)S(1)}, s32[48]{0:T(128)}, u32[]{:S(2)}) copy-start(s32[48]{0:T(128)} %fusion.116) | copy-start | bytes 580
  612.8 22.4 %all-to-all-start.3 = ((f32[64,1,192]{2,1,0:T(1,128)}), f32[64,1,192]{2,1,0:T(1,128)S(1)}, u32[]{:S(2)}, u32[]{:S(2)}) async-start(f32[64,1,192]{2,1,0:T(1,128)} %reshape.141), calls=%async_computation.3 | async-start | bytes 131072 | tf_op jit(solution)/shard_map/all_to_all | solution.py:111
  622.2 78.1 %all-reduce.5.cloned.1.call-start = ((), (), s32[]{:S(2)}) async-start(), calls=%async_computation.4 | async-start | bytes 262144 | tf_op jit(solution)/shard_map/psum | solution.py:72
  642.5 7.1 copy-start.13
Sparse Core Ops, SparseCore 0:
  331.8 184.1 all-reduce.6
Sparse Core Ops, SparseCore 1:
  625.6 74.6 all-reduce.4
where the time goes:
time: 720 us; the launch traced here: 710 us
  blocking collectives  294 us (41%)
  waiting for transfers between devices  241 us (33%)
  local copies, waits for them, and re-layouts  54.9 us (8%)
  matrix products  48.6 us (7%)
  starting transfers between devices  38.8 us (5%)
  between operations  17.9 us (2%)
  other arithmetic  14.9 us (2%)
    unnamed x1, blocking collectives  246 us
    unnamed x3, waiting for transfers between devices  181 us
    psum x1, waiting for transfers between devices, per_device(): density = lax.psum(density_part, 'band')  50 us
    all_gather x1, blocking collectives, per_device(): applied = lax.all_gather(mine, 'grid', axis=0, tiled=True)  48.1 us
    unnamed x53, local copies, waits for them, and re-layouts  31.6 us
    all_to_all x2, starting transfers between devices, per_device(): lax.all_to_all(columns[:, member:member + 1], 'grid', split_axis=3, conca...  22.2 us
    all_to_all x2, starting transfers between devices, per_device(): lax.all_to_all(picked[:, member:member + 1], 'grid', split_axis=2, concat...  16.3 us
  transfers between devices with their start and end apart: 6, of which 4 were waited for; matrix products, arithmetic and copies ran while one was open for 7% of the time, Pallas kernels for 0%

commit v1 on v0

v1 whole, which is shorter than its diff:
```python
import functools

import jax
import jax.numpy as jnp
import numpy as np
from jax import lax
from jax.experimental import pallas as pl
from jax.experimental.pallas import tpu as pltpu
from jax.sharding import PartitionSpec as P

MESH = pl.DeviceIdType.MESH
F32 = jnp.float32
BF16 = jnp.bfloat16
KINETIC = 0.0005

N = 128
BOX = 64
PLANES = 2
BANDS = 2
COLS = 48
SLOT = 64
PROJ = 18
PAIRS = 256
ATOMS = 8
COMBOS = 4
ROWS = PLANES * N


def split(table):
    high = table.astype(jnp.bfloat16)
    low = (table - high.astype(np.float64)).astype(jnp.bfloat16)
    return np.stack([high, low])


def tables(grid_count):
    scale = 1.0 / np.sqrt(N)
    pos = np.arange(N)
    box = np.arange(BOX)
    freq = np.where(box >= BOX // 2, box - BOX, box)

    def cos_sin(left, right):
        angle = 2.0 * np.pi / N * (np.outer(left, right) % N)
        return np.cos(angle) * scale, np.sin(angle) * scale

    cos_x, sin_x = cos_sin(pos, pos)
    x_table = np.zeros((grid_count, 2, PLANES, 2, N))
    cos_r = cos_x.reshape(grid_count, PLANES, N)
    sin_r = sin_x.reshape(grid_count, PLANES, N)
    x_table[:, 0, :, 0] = cos_r
    x_table[:, 0, :, 1] = -sin_r
    x_table[:, 1, :, 0] = sin_r
    x_table[:, 1, :, 1] = cos_r
    x_table = x_table.reshape(2 * N, 2 * N)
    cos_y, sin_y = cos_sin(freq, pos)
    y_table = np.zeros((BANDS, BOX, 2, BANDS, N))
    for band in range(BANDS):
        y_table[band, :, 0, band] = cos_y
        y_table[band, :, 1, band] = sin_y
    y_back = y_table.transpose(3, 4, 2, 0, 1).reshape(BANDS * N, 2 * BANDS * BOX)
    y_table = y_table.reshape(BANDS * BOX, 2 * BANDS * N)
    cos_z, sin_z = cos_sin(pos, freq)
    z_table = np.block([[cos_z, -sin_z], [sin_z, cos_z]])
    return [split(t) for t in (x_table, y_table, y_back, z_table, z_table.T)]


def halves(value):
    high = value.astype(BF16)
    low = (value - high.astype(F32)).astype(BF16)
    return high, low


def mm(left, right, dims=((1,), (0,))):
    return lax.dot_general(left, right, (dims, ((), ())), preferred_element_type=F32)


NT = ((1,), (1,))
TN = ((0,), (0,))


def iota(shape, dim):
    return lax.broadcasted_iota(jnp.int32, shape, dim)


def make_kernel(grid_count, band_count):
    peers = grid_count - 1
    half = grid_count // 2

    def kernel(
        psi_ref, col_ref, vloc_ref, proj_ref, atom_ref, row_ref, dmat_ref, occ_ref,
        xt_ref, yt_ref, yb_ref, zt_ref, zb_ref,
        out_ref, dens_ref,
        proj_buf, proj_t, psi_pad, msg1, got1, msg2, got2, code_y, code_z, oh_y, box_ref,
        field, tiles, coeff, near_coeff, near_atom, atom_col, vloc_t,
        d_own, d_mate, d_slot, d_send, summed, applied, added, h_ref,
        dens_loc, dens_part, dens_full, work,
        proj_sem, own_sem, s1, r1, s2, r2, sd, rd, sm, rm, sa, ra, sc, rc, sp, rp, sf, rf,
    ):
        me = lax.axis_index("grid")
        band = lax.axis_index("band")
        core = lax.rem(me, 2)
        chip = me // 2

        def to_grid(src, dst, send, recv, target):
            return pltpu.make_async_remote_copy(
                src_ref=src, dst_ref=dst, send_sem=send, recv_sem=recv,
                device_id={"grid": target}, device_id_type=MESH,
            )

        def to_band(src, dst, send, recv, target):
            return pltpu.make_async_remote_copy(
                src_ref=src, dst_ref=dst, send_sem=send, recv_sem=recv,
                device_id={"band": target}, device_id_type=MESH,
            )

        def settle(ref, sem):
            pltpu.make_async_copy(ref, ref, sem).wait()

        barrier = pltpu.get_barrier_semaphore()

        def greet_grid(step, carry):
            pl.semaphore_signal(
                barrier, inc=1, device_id={"grid": lax.rem(me + step, grid_count)},
                device_id_type=MESH,
            )
            return carry

        def greet_band(step, carry):
            pl.semaphore_signal(
                barrier, inc=1, device_id={"band": lax.rem(band + step, band_count)},
                device_id_type=MESH,
            )
            return carry

        proj_copy = pltpu.make_async_copy(proj_ref, proj_buf, proj_sem)
        proj_copy.start()
        lax.fori_loop(1, grid_count, greet_grid, 0)
        if band_count > 1:
            lax.fori_loop(1, band_count, greet_band, 0)

        psi_pad[...] = jnp.zeros_like(psi_pad)
        for member in range(BANDS):
            for part in range(2):
                psi_pad[member * SLOT : member * SLOT + COLS, part * N : (part + 1) * N] = psi_ref[
                    part, member
                ]
        psi_hi, psi_lo = halves(psi_pad[...])
        spread = mm(xt_ref[0], psi_hi, NT) + mm(xt_ref[1], psi_hi, NT) + mm(xt_ref[0], psi_lo, NT)
        work[...] = jnp.zeros_like(work)
        work[0:1, 0:COLS] = col_ref[...].astype(F32)
        codes = jnp.broadcast_to(work[0:1, :], (8, N))
        sub = iota((8, N), 0) % 4
        lane = iota((8, N), 1)
        pattern = jnp.where(
            sub == 0,
            pltpu.roll(codes, 48, 1),
            jnp.where(sub == 1, pltpu.roll(codes, 32, 1), pltpu.roll(codes, 16, 1)),
        )
        pattern = jnp.where((lane >= COLS) & (lane < SLOT) & (sub < 3), pattern, 0.0)
        for pair in range(grid_count // 2):
            both = spread[8 * pair : 8 * pair + 8] + pattern
            msg1[2 * pair] = both[0:4]
            msg1[2 * pair + 1] = both[4:8]
        got1[me] = msg1[me]
        for q in range(3):
            d_send[q] = dmat_ref[q]
        d_own[chip] = d_send[...]

        pl.semaphore_wait(barrier, peers + band_count - 1)

        def send1(step, carry):
            target = lax.rem(me + step, grid_count)
            to_grid(msg1.at[target], got1.at[me], s1, r1, target).start()
            return carry

        lax.fori_loop(1, grid_count, send1, 0)
        near = [lax.rem(me + off + grid_count, grid_count) for off in (1, -1, 2, -2)]
        atom_copies = [
            to_grid(atom_ref, near_atom.at[i], sa.at[i], ra.at[i], near[i]) for i in range(4)
        ]
        for copy in atom_copies:
            copy.start()

        def send_d(step, carry):
            other = lax.rem(chip + step, half)
            to_grid(d_send, d_own.at[chip], sd, rd, 2 * other + core).start()
            return carry

        lax.fori_loop(1, half, send_d, 0)

        for plane in range(PLANES):
            vloc_t[:, plane * N : (plane + 1) * N] = vloc_ref[plane].T
        atom_row = atom_ref[...].astype(F32)
        for part in range(2):
            atom_col[part * N : (part + 1) * N, :] = jnp.broadcast_to(
                atom_row[:, part * N : (part + 1) * N], (N, N)
            ).T
        proj_copy.wait()
        for i in range(PROJ):
            for part in range(2):
                proj_t[i, :, part * N : (part + 1) * N] = proj_buf[
                    part * N : (part + 1) * N, i, :
                ].T

        settle(got1.at[pl.ds(0, peers)], r1)
        rows = [got1[:, r, :] for r in range(3)]
        wide = iota((grid_count, N), 1)
        low = wide % SLOT
        code = jnp.where(
            low < 16,
            pltpu.roll(rows[0], 80, 1),
            jnp.where(low < 32, pltpu.roll(rows[1], 96, 1), pltpu.roll(rows[2], 112, 1)),
        )
        code = jnp.where(wide < SLOT, code, pltpu.roll(code, SLOT, 1)).astype(jnp.int32)
        valid = low < COLS
        code_y[...] = jnp.where(valid, ((code // N) % BOX) + jnp.where(wide < SLOT, 0, BOX), -1)
        code_z[...] = jnp.where(valid, code % BOX, -1)

        box_ref[...] = jnp.zeros_like(box_ref)
        row_id = iota((BANDS * BOX, N), 0)
        z_id = iota((BOX, N), 0)

        def fill(chunk, carry):
            base = pl.multiple_of(chunk * 8, 8)
            ys = code_y[pl.ds(base, 8), :]
            zs = code_z[pl.ds(base, 8), :]
            total = jnp.zeros((2 * PLANES * BOX, BANDS * BOX), F32)
            for pair in range(4):
                picks, highs, lows = [], [], []
                for j in (2 * pair, 2 * pair + 1):
                    picker = jnp.where(row_id == ys[j : j + 1], 1.0, 0.0).astype(BF16)
                    oh_y[base + j] = picker
                    picks.append(picker)
                    data = got1[base + j]
                    high = data.astype(BF16).astype(F32)
                    rest = data - high
                    at = z_id == zs[j : j + 1]
                    highs.append(
                        jnp.concatenate(
                            [jnp.where(at, high[r : r + 1], 0.0) for r in range(4)], axis=0
                        ).astype(BF16)
                    )
                    lows.append(
                        jnp.concatenate(
                            [jnp.where(at, rest[r : r + 1], 0.0) for r in range(4)], axis=0
                        ).astype(BF16)
                    )
                pick = jnp.concatenate(picks, axis=1)
                total += mm(jnp.concatenate(highs, axis=1), pick, NT)
                total += mm(jnp.concatenate(lows, axis=1), pick, NT)
            box_ref[...] += total
            return carry

        lax.fori_loop(0, grid_count // 8, fill, 0)

        box_hi, box_lo = halves(box_ref[...])
        turned = mm(box_hi, yt_ref[0]) + mm(box_lo, yt_ref[0]) + mm(box_hi, yt_ref[1])
        mid, end = PLANES * BOX, BANDS * N
        part_re = turned[:mid, :end] - turned[mid:, end:]
        part_im = turned[:mid, end:] + turned[mid:, :end]
        for plane in range(PLANES):
            here = slice(plane * BOX, (plane + 1) * BOX)
            value = jnp.concatenate([part_re[here], part_im[here]], axis=0)
            v_hi, v_lo = halves(value)
            wave = mm(zt_ref[0], v_hi) + mm(zt_ref[1], v_hi) + mm(zt_ref[0], v_lo)
            for part in range(2):
                for member in range(BANDS):
                    first = (part * BANDS + member) * N
                    field[first : first + N, plane * N : (plane + 1) * N] = wave[
                        part * N : (part + 1) * N, member * N : (member + 1) * N
                    ]

        dens_t = jnp.zeros((N, ROWS), F32)
        for member in range(BANDS):
            real = field[member * N : (member + 1) * N, :]
            imag = field[(BANDS + member) * N : (BANDS + member + 1) * N, :]
            dens_t += occ_ref[0, member] * (real * real + imag * imag)
        for plane in range(PLANES):
            dens_loc[plane * N : (plane + 1) * N, :] = dens_t[:, plane * N : (plane + 1) * N].T
        share = ROWS // band_count

        def send_part(step, carry):
            target = lax.rem(band + step, band_count)
            first = pl.multiple_of(target * share, share)
            to_band(dens_loc.at[pl.ds(first, share)], dens_part.at[band], sp, rp, target).start()
            return carry

        if band_count > 1:
            lax.fori_loop(1, band_count, send_part, 0)

        local_row = row_ref[...] - me * ROWS
        row_pick = jnp.where(iota((ROWS, PAIRS), 0) == local_row, 1.0, 0.0).astype(BF16)
        f_hi, f_lo = halves(field[...])
        tiles[...] = mm(f_hi, row_pick) + mm(f_lo, row_pick)

        def project(step, carry):
            found = []
            for k in range(2):
                values = proj_t[2 * step + k]
                for combo in range(COMBOS):
                    found.append(
                        jnp.sum(values * tiles[combo * N : (combo + 1) * N, :], axis=0, keepdims=True)
                    )
            coeff[pl.ds(pl.multiple_of(step * 8, 8), 8), :] = jnp.concatenate(found, axis=0)
            return carry

        lax.fori_loop(0, PROJ // 2, project, 0)
        coeff_copies = [
            to_grid(coeff, near_coeff.at[i], sc.at[i], rc.at[i], near[i]) for i in range(4)
        ]
        for copy in coeff_copies:
            copy.start()

        if band_count > 1:
            settle(dens_part.at[pl.ds(0, band_count - 1)], rp)
        mine = pl.ds(pl.multiple_of(band * share, share), share)
        dens_part[band] = dens_loc[mine, :]
        whole = dens_part[0]
        for other in range(1, band_count):
            whole += dens_part[other]
        dens_full[mine, :] = whole

        def send_full(step, carry):
            target = lax.rem(band + step, band_count)
            to_band(dens_full.at[mine], dens_full.at[mine], sf, rf, target).start()
            return carry

        if band_count > 1:
            lax.fori_loop(1, band_count, send_full, 0)

        settle(d_own.at[pl.ds(0, half - 1)], rd)
        mate = to_grid(d_own, d_mate, sm, rm, 2 * chip + 1 - core)
        mate.start()
        place = iota((half * ATOMS, PAIRS), 0)
        atom_base = (place // ATOMS) * (2 * ATOMS) + place % ATOMS
        atoms = atom_ref[...]
        own_pick = jnp.where(atom_base + core * ATOMS == atoms, 1.0, 0.0).astype(BF16)
        mate_pick = jnp.where(atom_base + (1 - core) * ATOMS == atoms, 1.0, 0.0).astype(BF16)
        for q in range(3):
            d_hi, d_lo = halves(d_own[:, q].reshape(half * ATOMS, N))
            d_slot[q * N : (q + 1) * N, :] = mm(d_hi, own_pick, TN) + mm(d_lo, own_pick, TN)
        mate.wait_recv()
        for q in range(3):
            d_hi, d_lo = halves(d_mate[:, q].reshape(half * ATOMS, N))
            d_slot[q * N : (q + 1) * N, :] += mm(d_hi, mate_pick, TN) + mm(d_lo, mate_pick, TN)

        for copy in atom_copies:
            copy.wait_recv()
        column = jnp.concatenate([atom_col[...], atom_col[...]], axis=1)

        def same(other_row):
            return jnp.where(column == other_row.astype(F32), 1.0, 0.0).astype(BF16)

        c_hi, c_lo = halves(coeff[...])
        pick = same(atoms)
        total = mm(c_hi, pick, NT) + mm(c_lo, pick, NT)
        for i in range(4):
            coeff_copies[i].wait_recv()
            c_hi, c_lo = halves(near_coeff[i])
            pick = same(near_atom[i])
            total += mm(c_hi, pick, NT) + mm(c_lo, pick, NT)
        summed[...] = total

        for combo in range(COMBOS):
            value = jnp.zeros((PROJ, PAIRS), F32)
            for j in range(PROJ):
                first = (j // 7) * N + (j % 7) * PROJ
                value += d_slot[first : first + PROJ, :] * summed[
                    j * COMBOS + combo : j * COMBOS + combo + 1, :
                ]
            applied[combo, 0:PROJ, :] = value

        depth = 32

        def spread_back(step, carry):
            first = pl.multiple_of(step * depth, depth)
            totals = [jnp.zeros((depth, PAIRS), F32) for _ in range(COMBOS)]
            for i in range(PROJ):
                values = proj_t[i, pl.ds(first, depth), :]
                for combo in range(COMBOS):
                    totals[combo] += values * applied[combo, i : i + 1, :]
            for combo in range(COMBOS):
                added[pl.ds(pl.multiple_of(combo * N + first, depth), depth), :] = totals[combo]
            return carry

        lax.fori_loop(0, N // depth, spread_back, 0)
        a_hi, a_lo = halves(added[...])
        projected = mm(a_hi, row_pick, NT) + mm(a_lo, row_pick, NT)
        for combo in range(COMBOS):
            here = slice(combo * N, (combo + 1) * N)
            h_ref[here, :] = vloc_t[...] * field[here, :] + projected[here]

        spectra = []
        for plane in range(PLANES):
            lanes = slice(plane * N, (plane + 1) * N)
            value = jnp.concatenate(
                [
                    jnp.concatenate(
                        [
                            h_ref[(part * BANDS + member) * N : (part * BANDS + member + 1) * N, lanes]
                            for member in range(BANDS)
                        ],
                        axis=1,
                    )
                    for part in range(2)
                ],
                axis=0,
            )
            v_hi, v_lo = halves(value)
            spectra.append(mm(zb_ref[0], v_hi) + mm(zb_ref[1], v_hi) + mm(zb_ref[0], v_lo))
        turned = jnp.concatenate(
            [spectra[plane][part * BOX : (part + 1) * BOX] for part in range(2) for plane in range(PLANES)],
            axis=0,
        )
        t_hi, t_lo = halves(turned)
        turned = mm(t_hi, yb_ref[0]) + mm(t_lo, yb_ref[0]) + mm(t_hi, yb_ref[1])
        end = BANDS * BOX
        final = jnp.concatenate(
            [turned[:mid, :end] + turned[mid:, end:], turned[mid:, :end] - turned[:mid, end:]], axis=0
        )
        q_hi, q_lo = halves(final)
        both = jnp.concatenate([q_hi, q_lo], axis=1)

        def take(target):
            picker = oh_y[target]
            found = mm(both, jnp.concatenate([picker, picker], axis=0))
            at = z_id == code_z[pl.ds(target, 1), :]
            msg2[target] = jnp.concatenate(
                [
                    jnp.sum(
                        jnp.where(at, found[r * BOX : (r + 1) * BOX], 0.0), axis=0, keepdims=True
                    )
                    for r in range(4)
                ],
                axis=0,
            )

        def send2(step, carry):
            target = lax.rem(me + step, grid_count)
            take(target)
            to_grid(msg2.at[target], got2.at[me], s2, r2, target).start()
            return carry

        lax.fori_loop(1, grid_count, send2, 0)
        take(me)
        got2[me] = msg2[me]

        if band_count > 1:
            settle(dens_full.at[pl.ds(0, ROWS - share)], rf)
        dens_ref[...] = dens_full[...]
        first_freq = col_ref[...]

        work[...] = jnp.zeros_like(work)
        work[0:1, 0:COLS] = first_freq.astype(F32)
        codes = jnp.broadcast_to(work[0:1, :], (N, N)).T.astype(jnp.int32)[0:COLS]

        def signed(index):
            return jnp.where(index >= N // 2, index - N, index)

        fy, fz, fx = signed(codes // N), signed(codes % N), signed(iota((COLS, N), 1))
        kinetic = KINETIC * (fx * fx + fy * fy + fz * fz).astype(F32)

        settle(got2.at[pl.ds(0, peers)], r2)
        back = got2[...].reshape(grid_count * 4, N).T
        b_hi, b_lo = halves(back)
        result = mm(b_hi, xt_ref[0]) + mm(b_lo, xt_ref[0]) + mm(b_hi, xt_ref[1])
        for part in range(2):
            for member in range(BANDS):
                out_ref[part, member] = (
                    result[member * SLOT : member * SLOT + COLS, part * N : (part + 1) * N]
                    + kinetic * psi_ref[part, member]
                )

        settle(msg1.at[pl.ds(0, peers)], s1)
        settle(msg2.at[pl.ds(0, peers)], s2)
        settle(d_own.at[pl.ds(0, half - 1)], sd)
        mate.wait_send()
        for copy in atom_copies + coeff_copies:
            copy.wait_send()
        if band_count > 1:
            settle(dens_part.at[pl.ds(0, band_count - 1)], sp)
            settle(dens_full.at[pl.ds(0, ROWS - share)], sf)

    return kernel


def solution(mesh):
    grid_count = mesh.shape["grid"]
    band_count = mesh.shape["band"]
    half = grid_count // 2
    constants = tables(grid_count)

    def step(psi_g, col_index, v_local, proj_values, pair_atom, pair_row, d_matrices, occupations):
        d_flat = d_matrices.transpose(0, 2, 1)
        d_flat = jnp.pad(d_flat, ((0, 0), (0, 3), (0, 0))).reshape(ATOMS, 3, 7 * PROJ)
        d_flat = jnp.pad(d_flat, ((0, 0), (0, 0), (0, N - 7 * PROJ))).transpose(1, 0, 2)
        vmem = pl.BlockSpec(memory_space=pltpu.VMEM)
        dma = pltpu.SemaphoreType.DMA
        out, dens = pl.pallas_call(
            make_kernel(grid_count, band_count),
            out_shape=(
                jax.ShapeDtypeStruct(psi_g.shape, F32),
                jax.ShapeDtypeStruct((ROWS, N), F32),
            ),
            in_specs=[
                vmem, vmem, vmem, pl.BlockSpec(memory_space=pl.ANY), vmem, vmem, vmem,
                pl.BlockSpec(memory_space=pltpu.SMEM),
            ]
            + [vmem] * 5,
            out_specs=(vmem, vmem),
            scratch_shapes=[
                pltpu.VMEM((PAIRS, PROJ, N), F32),
                pltpu.VMEM((PROJ, N, PAIRS), F32),
                pltpu.VMEM((BANDS * SLOT, 2 * N), F32),
                pltpu.VMEM((grid_count, 4, N), F32),
                pltpu.VMEM((grid_count, 4, N), F32),
                pltpu.VMEM((grid_count, 4, N), F32),
                pltpu.VMEM((grid_count, 4, N), F32),
                pltpu.VMEM((grid_count, N), jnp.int32),
                pltpu.VMEM((grid_count, N), jnp.int32),
                pltpu.VMEM((grid_count, BANDS * BOX, N), BF16),
                pltpu.VMEM((2 * PLANES * BOX, BANDS * BOX), F32),
                pltpu.VMEM((COMBOS * N, ROWS), F32),
                pltpu.VMEM((COMBOS * N, PAIRS), F32),
                pltpu.VMEM((PROJ * COMBOS, PAIRS), F32),
                pltpu.VMEM((4, PROJ * COMBOS, PAIRS), F32),
                pltpu.VMEM((4, 1, PAIRS), jnp.int32),
                pltpu.VMEM((PAIRS, N), F32),
                pltpu.VMEM((N, ROWS), F32),
                pltpu.VMEM((half, 3, ATOMS, N), F32),
                pltpu.VMEM((half, 3, ATOMS, N), F32),
                pltpu.VMEM((3 * N, PAIRS), F32),
                pltpu.VMEM((3, ATOMS, N), F32),
                pltpu.VMEM((PROJ * COMBOS, PAIRS), F32),
                pltpu.VMEM((COMBOS, 24, PAIRS), F32),
                pltpu.VMEM((COMBOS * N, PAIRS), F32),
                pltpu.VMEM((COMBOS * N, ROWS), F32),
                pltpu.VMEM((ROWS, N), F32),
                pltpu.VMEM((band_count, ROWS // band_count, N), F32),
                pltpu.VMEM((ROWS, N), F32),
                pltpu.VMEM((8, N), F32),
                dma, dma, dma, dma, dma, dma, dma, dma, dma, dma,
                dma((4,)), dma((4,)), dma((4,)), dma((4,)), dma, dma, dma, dma,
            ],
            compiler_params=pltpu.CompilerParams(
                collective_id=0, has_side_effects=True, vmem_limit_bytes=48 << 20
            ),
        )(
            psi_g,
            col_index.reshape(1, COLS),
            v_local,
            proj_values,
            pair_atom.reshape(1, PAIRS),
            pair_row.reshape(1, PAIRS),
            d_flat,
            occupations.reshape(1, BANDS),
            *[jnp.asarray(t) for t in constants],
        )
        return out, dens.reshape(PLANES, N, N)

    return jax.shard_map(
        step,
        mesh=mesh,
        in_specs=(
            P(None, "band", "grid", None),
            P("grid"),
            P("grid", None, None),
            P("grid", None, None),
            P("grid"),
            P("grid"),
            P("grid", None, None),
            P("band"),
        ),
        out_specs=(P(None, "band", "grid", None), P("grid", None, None)),
        check_vma=False,
    )
```

time: 720 us -> 62 us (0.09); the launches traced: 710 us -> 61.8 us
  blocking collectives: 294 us -> 0 us
  waiting for transfers between devices: 241 us -> 0 us
  Pallas kernels: 0 us -> 55.3 us
  local copies, waits for them, and re-layouts: 54.9 us -> 5.68 us
  matrix products: 48.6 us -> 0 us
  starting transfers between devices: 38.8 us -> 0 us
  between operations: 17.9 us -> 0.84 us
  other arithmetic: 14.9 us -> 0 us
    unnamed x1 -> x0, blocking collectives: 246 us -> none
    unnamed x3 -> x0, waiting for transfers between devices: 181 us -> none
    pallas_call x0 -> x1, Pallas kernels: none -> 55.3 us  [step(): pl.pallas_call(make_kernel(grid_count, band_count), out_shape=(jax.ShapeD...]
    psum x1 -> x0, waiting for transfers between devices: 50 us -> none  [per_device(): density = lax.psum(density_part, 'band')]
    dot_general x27 -> x0, matrix products: 48.6 us -> none  [the longest x1 7.39 us: per_device(): jnp.einsum('piz,cbpz->picb', proj_values, tiles, precision=HIGH)]
    all_gather x1 -> x0, blocking collectives: 48.1 us -> none  [per_device(): applied = lax.all_gather(mine, 'grid', axis=0, tiled=True)]
    all_to_all x4 -> x0, starting transfers between devices: 38.5 us -> none  [the longest x2 22.2 us: per_device(): lax.all_to_all(columns[:, member:member + 1], 'grid', split_axis=3, conca...]
    unnamed x53 -> x26, local copies, waits for them, and re-layouts: 31.6 us -> 5.56 us
  transfers between devices with their start and end apart: 6 -> 0, of which waited for: 4 -> 0; matrix products, arithmetic and copies ran while one was open for 7% -> 0% of each run, Pallas kernels for 0% -> 0%
where the time goes in v1:
time: 62 us; the launch traced here: 61.8 us
  Pallas kernels  55.3 us (89%)
  local copies, waits for them, and re-layouts  5.68 us (9%)
  between operations  0.84 us (1%)
    pallas_call x1, Pallas kernels, step(): pl.pallas_call(make_kernel(grid_count, band_count), out_shape=(jax.ShapeD...  55.3 us
    unnamed x26, local copies, waits for them, and re-layouts  5.56 us

profile of v1, /device:TPU:1, one launch (start us, length us, event | category | flops | bytes accessed | tf_op | source)
XLA Modules:
  0.0 61.8 jit_solution(8681043533828662520)
XLA Ops:
  0.6 0.0 copy-start.4
  0.6 0.0 copy-start.5
  0.7 0.0 copy-start
  0.7 0.0 copy-start.1
  0.7 0.0 copy-start.2
  0.7 0.0 copy-start.10
  0.7 0.0 copy-start.8
  0.7 0.0 copy-start.7
  0.7 0.0 copy-start.3
  0.7 0.0 copy-start.9
  0.7 0.0 copy-start.6
  0.8 1.1 %copy.19 = f32[8,18,18]{2,1,0:T(8,128)S(1)} copy(f32[8,18,18]{1,0,2:T(8,128)} %bitcast.13) | data formatting | bytes 20736
  1.9 0.1 reshape.25
  2.0 3.1 %copy.18.proj_ref = f32[256,18,128]{2,1,0:T(8,128)S(1)} copy(f32[256,18,128]{2,0,1:T(8,128)} %param.16) | data formatting | bytes 4718592 | tf_op args[3]
  5.1 0.0 copy-done.4
  5.1 0.0 copy-done.5
  5.1 0.0 copy-done
  5.1 0.0 copy-done.1
  5.1 0.0 copy-done.2
  5.1 0.0 copy-done.10
  5.2 0.0 copy-done.8
  5.2 0.0 copy-done.7
  5.2 0.0 copy-done.3
  5.2 0.0 copy-done.9
  5.2 0.0 copy-done.6
  5.2 55.3 %shard_map.140 = (f32[2,2,48,128]{3,2,1,0:T(8,128)S(1)}, f32[256,128]{1,0:T(8,128)S(1)}) custom-call(f32[2,2,48,128]{3,2,1,0:T(8,128)S(1)} %copy-done.6, s32[1,48]{1,0:T(1,128)S(1)} %bitcast.11, f32[2,128,128]{2,1,0:T(8,128)S(1)} %copy-done.3, f32[256,18,128]{2,1,0:T(8,128)S(1)} %copy.18.proj_ref, s32[1,256]{1,0:T(1,128)S(1)} %bitcast.9, ...), custom_call_target="tpu_custom_call" | custom-call | tf_op jit(solution)/shard_map/pallas_call | solution.py:498
  60.5 0.6 %copy.22 = f32[2,2,48,128]{3,2,1,0:T(8,128)} copy(f32[2,2,48,128]{3,2,1,0:T(8,128)S(1)} %get-tuple-element.8) | data formatting | bytes 196608
  61.1 0.7 %copy.23 = f32[2,128,128]{2,1,0:T(8,128)} copy(f32[2,128,128]{2,1,0:T(8,128)S(1)} %bitcast.8) | data formatting | bytes 262144
  (3 shorter events, 0.0 us)
Async XLA Ops:
  0.6 4.5 %copy-start.4 = (bf16[2,128,256]{2,1,0:T(8,128)(2,1)S(1)}, bf16[2,128,256]{2,1,0:T(8,128)(2,1)}, u32[]{:S(2)}) copy-start(bf16[2,128,256]{2,1,0:T(8,128)(2,1)} %constant.17.clone.zb_ref) | copy-start | bytes 393220
  0.6 4.5 %copy-start.5 = (bf16[2,256,128]{2,1,0:T(8,128)(2,1)S(1)}, bf16[2,256,128]{2,1,0:T(8,128)(2,1)}, u32[]{:S(2)}) copy-start(bf16[2,256,128]{2,1,0:T(8,128)(2,1)} %constant.16.clone.zt_ref) | copy-start | bytes 393220
  0.7 4.5 %copy-start = (bf16[2,256,256]{2,1,0:T(8,128)(2,1)S(1)}, bf16[2,256,256]{2,1,0:T(8,128)(2,1)}, u32[]{:S(2)}) copy-start(bf16[2,256,256]{2,1,0:T(8,128)(2,1)} %constant.15.clone.yb_ref) | copy-start | bytes 786436
  0.7 4.5 %copy-start.1 = (bf16[2,128,512]{2,1,0:T(8,128)(2,1)S(1)}, bf16[2,128,512]{2,1,0:T(8,128)(2,1)}, u32[]{:S(2)}) copy-start(bf16[2,128,512]{2,1,0:T(8,128)(2,1)} %constant.14.clone.yt_ref) | copy-start | bytes 786436
  0.7 4.5 %copy-start.2 = (bf16[2,256,256]{2,1,0:T(8,128)(2,1)S(1)}, bf16[2,256,256]{2,1,0:T(8,128)(2,1)}, u32[]{:S(2)}) copy-start(bf16[2,256,256]{2,1,0:T(8,128)(2,1)} %constant.13.clone.xt_ref) | copy-start | bytes 786436
  0.7 4.5 %copy-start.10 = (f32[2]{0:T(128)S(1)}, f32[2]{0:T(128)}, u32[]{:S(2)}) copy-start(f32[2]{0:T(128)} %param.20) | copy-start | bytes 28
  0.7 4.5 %copy-start.8 = (s32[256]{0:T(256)S(1)}, s32[256]{0:T(256)}, u32[]{:S(2)}) copy-start(s32[256]{0:T(256)} %param.18) | copy-start | bytes 3076
  0.7 4.5 %copy-start.7 = (s32[256]{0:T(256)S(1)}, s32[256]{0:T(256)}, u32[]{:S(2)}) copy-start(s32[256]{0:T(256)} %param.17) | copy-start | bytes 3076
  0.7 4.5 %copy-start.3 = (f32[2,128,128]{2,1,0:T(8,128)S(1)}, f32[2,128,128]{2,1,0:T(8,128)}, u32[]{:S(2)}) copy-start(f32[2,128,128]{2,1,0:T(8,128)} %vloc_ref.1) | copy-start | bytes 393220
  0.7 4.5 %copy-start.9 = (s32[48]{0:T(128)S(1)}, s32[48]{0:T(128)}, u32[]{:S(2)}) copy-start(s32[48]{0:T(128)} %param.14) | copy-start | bytes 580
  0.7 4.5 %copy-start.6 = (f32[2,2,48,128]{3,2,1,0:T(8,128)S(1)}, f32[2,2,48,128]{3,2,1,0:T(8,128)}, u32[]{:S(2)}) copy-start(f32[2,2,48,128]{3,2,1,0:T(8,128)} %psi_ref.1) | copy-start | bytes 294916

commit v2 on v1

--- a/solution.py
+++ b/solution.py
@@ -86,14 +86,15 @@
     half = grid_count // 2
 
     def kernel(
-        psi_ref, col_ref, vloc_ref, proj_ref, atom_ref, row_ref, dmat_ref, occ_ref,
-        xt_ref, yt_ref, yb_ref, zt_ref, zb_ref,
-        out_ref, dens_ref,
-        proj_buf, proj_t, psi_pad, msg1, got1, msg2, got2, code_y, code_z, oh_y, box_ref,
+        psi_in, col_in, xt_in, dmat_in, atom_in, vloc_in, proj_in, row_in, yt_in, zt_in, zb_in,
+        yb_in, occ_ref,
+        out_hbm, dens_hbm,
+        psi_ref, col_ref, xt_ref, dmat_ref, atom_ref, vloc_ref, proj_buf, row_ref, yt_ref, zt_ref,
+        zb_ref, yb_ref, out_ref, proj_t, psi_pad, msg1, got1, msg2, got2, code_z, oh_y, box_ref,
         field, tiles, coeff, near_coeff, near_atom, atom_col, vloc_t,
         d_own, d_mate, d_slot, d_send, summed, applied, added, h_ref,
         dens_loc, dens_part, dens_full, work,
-        proj_sem, own_sem, s1, r1, s2, r2, sd, rd, sm, rm, sa, ra, sc, rc, sp, rp, sf, rf,
+        in_sem, out_sem, s1, r1, s2, r2, sd, rd, sm, rm, sa, ra, sc, rc, sp, rp, sf, rf,
     ):
         me = lax.axis_index("grid")
         band = lax.axis_index("band")
@@ -115,6 +116,9 @@
         def settle(ref, sem):
             pltpu.make_async_copy(ref, ref, sem).wait()
 
+        def far(step):
+            return half + (1 - 2 * (step % 2)) * ((step + 1) // 2)
+
         barrier = pltpu.get_barrier_semaphore()
 
         def greet_grid(step, carry):
@@ -131,13 +135,26 @@
             )
             return carry
 
-        proj_copy = pltpu.make_async_copy(proj_ref, proj_buf, proj_sem)
-        proj_copy.start()
+        inputs = [
+            pltpu.make_async_copy(src, dst, in_sem.at[i])
+            for i, (src, dst) in enumerate(
+                [
+                    (psi_in, psi_ref), (col_in, col_ref), (xt_in, xt_ref), (dmat_in, dmat_ref),
+                    (atom_in, atom_ref), (vloc_in, vloc_ref), (proj_in, proj_buf),
+                    (row_in, row_ref), (yt_in, yt_ref), (zt_in, zt_ref), (zb_in, zb_ref),
+                    (yb_in, yb_ref),
+                ]
+            )
+        ]
+        for copy in inputs:
+            copy.start()
         lax.fori_loop(1, grid_count, greet_grid, 0)
         if band_count > 1:
             lax.fori_loop(1, band_count, greet_band, 0)
 
         psi_pad[...] = jnp.zeros_like(psi_pad)
+        for copy in inputs[:4]:
+            copy.wait()
         for member in range(BANDS):
             for part in range(2):
                 psi_pad[member * SLOT : member * SLOT + COLS, part * N : (part + 1) * N] = psi_ref[
@@ -160,20 +177,24 @@
             both = spread[8 * pair : 8 * pair + 8] + pattern
             msg1[2 * pair] = both[0:4]
             msg1[2 * pair + 1] = both[4:8]
-        got1[me] = msg1[me]
-        for q in range(3):
-            d_send[q] = dmat_ref[q]
+        own_copy = pltpu.make_async_copy(msg1.at[me], got1.at[me], r1.at[grid_count // 8 - 1])
+        own_copy.start()
+        d_send[...] = jnp.zeros_like(d_send)
+        for i in range(PROJ):
+            first = (i % 7) * PROJ
+            d_send[i // 7, :, first : first + PROJ] = dmat_ref[i]
         d_own[chip] = d_send[...]
 
         pl.semaphore_wait(barrier, peers + band_count - 1)
 
         def send1(step, carry):
-            target = lax.rem(me + step, grid_count)
-            to_grid(msg1.at[target], got1.at[me], s1, r1, target).start()
-            return carry
-
-        lax.fori_loop(1, grid_count, send1, 0)
+            target = lax.rem(me + far(step), grid_count)
+            to_grid(msg1.at[target], got1.at[me], s1, r1.at[step // 8], target).start()
+            return carry
+
+        lax.fori_loop(0, peers, send1, 0)
         near = [lax.rem(me + off + grid_count, grid_count) for off in (1, -1, 2, -2)]
+        inputs[4].wait()
         atom_copies = [
             to_grid(atom_ref, near_atom.at[i], sa.at[i], ra.at[i], near[i]) for i in range(4)
         ]
@@ -187,6 +208,7 @@
 
         lax.fori_loop(1, half, send_d, 0)
 
+        inputs[5].wait()
         for plane in range(PLANES):
             vloc_t[:, plane * N : (plane + 1) * N] = vloc_ref[plane].T
         atom_row = atom_ref[...].astype(F32)
@@ -194,56 +216,55 @@
             atom_col[part * N : (part + 1) * N, :] = jnp.broadcast_to(
                 atom_row[:, part * N : (part + 1) * N], (N, N)
             ).T
-        proj_copy.wait()
+        inputs[6].wait()
         for i in range(PROJ):
             for part in range(2):
-                proj_t[i, :, part * N : (part + 1) * N] = proj_buf[
-                    part * N : (part + 1) * N, i, :
-                ].T
-
-        settle(got1.at[pl.ds(0, peers)], r1)
-        rows = [got1[:, r, :] for r in range(3)]
-        wide = iota((grid_count, N), 1)
-        low = wide % SLOT
-        code = jnp.where(
-            low < 16,
-            pltpu.roll(rows[0], 80, 1),
-            jnp.where(low < 32, pltpu.roll(rows[1], 96, 1), pltpu.roll(rows[2], 112, 1)),
-        )
-        code = jnp.where(wide < SLOT, code, pltpu.roll(code, SLOT, 1)).astype(jnp.int32)
-        valid = low < COLS
-        code_y[...] = jnp.where(valid, ((code // N) % BOX) + jnp.where(wide < SLOT, 0, BOX), -1)
-        code_z[...] = jnp.where(valid, code % BOX, -1)
+                proj_t[i, :, part * N : (part + 1) * N] = proj_buf[i, part * N : (part + 1) * N, :].T
 
         box_ref[...] = jnp.zeros_like(box_ref)
         row_id = iota((BANDS * BOX, N), 0)
         z_id = iota((BOX, N), 0)
-
-        def fill(chunk, carry):
-            base = pl.multiple_of(chunk * 8, 8)
-            ys = code_y[pl.ds(base, 8), :]
-            zs = code_z[pl.ds(base, 8), :]
+        sub = iota((8, N), 0)
+        lane = iota((8, N), 1)
+        code_place = lane // 16 == (sub + 3) % 8
+        lane = iota((1, N), 1)
+        filled = lane % SLOT < COLS
+        upper = lane >= SLOT
+
+        def fill(step, carry):
+            group = grid_count // 8 - 1 - step
+            settle(got1.at[pl.ds(0, 8)], r1.at[group])
             total = jnp.zeros((2 * PLANES * BOX, BANDS * BOX), F32)
             for pair in range(4):
+                senders = [
+                    lax.rem(me + grid_count - far(8 * group + 2 * pair + k), grid_count)
+                    for k in range(2)
+                ]
+                data = [got1[sender] for sender in senders]
+                codes = pltpu.roll(jnp.concatenate(data, axis=0), 0, 1, stride=16, stride_axis=0)
+                codes = jnp.where(code_place, codes, 0.0)
                 picks, highs, lows = [], [], []
-                for j in (2 * pair, 2 * pair + 1):
-                    picker = jnp.where(row_id == ys[j : j + 1], 1.0, 0.0).astype(BF16)
-                    oh_y[base + j] = picker
+                for k in range(2):
+                    code = jnp.sum(codes[4 * k : 4 * k + 4], axis=0, keepdims=True)
+                    code = jnp.broadcast_to(code, (8, N))
+                    turned = [pltpu.roll(code, 80, 1), pltpu.roll(code, 16, 1)]
+                    code = jnp.where(upper, turned[1 - k], turned[k])[0:1]
+                    code = code.astype(jnp.int32)
+                    at_y = jnp.where(filled, (code // N) % BOX + jnp.where(upper, BOX, 0), -1)
+                    at_z = jnp.where(filled, code % BOX, -1)
+                    code_z[senders[k]] = at_z
+                    picker = jnp.where(row_id == at_y, 1.0, 0.0).astype(BF16)
+                    oh_y[senders[k]] = picker
                     picks.append(picker)
-                    data = got1[base + j]
-                    high = data.astype(BF16).astype(F32)
-                    rest = data - high
-                    at = z_id == zs[j : j + 1]
-                    highs.append(
-                        jnp.concatenate(
-                            [jnp.where(at, high[r : r + 1], 0.0) for r in range(4)], axis=0
-                        ).astype(BF16)
-                    )
-                    lows.append(
-                        jnp.concatenate(
-                            [jnp.where(at, rest[r : r + 1], 0.0) for r in range(4)], axis=0
-                        ).astype(BF16)
-                    )
+                    high = data[k].astype(BF16).astype(F32)
+                    rest = data[k] - high
+                    at = z_id == at_z
+                    for value, store in ((high, highs), (rest, lows)):
+                        store.append(
+                            jnp.concatenate(
+                                [jnp.where(at, value[r : r + 1], 0.0) for r in range(4)], axis=0
+                            ).astype(BF16)
+                        )
                 pick = jnp.concatenate(picks, axis=1)
                 total += mm(jnp.concatenate(highs, axis=1), pick, NT)
                 total += mm(jnp.concatenate(lows, axis=1), pick, NT)
@@ -252,6 +273,8 @@
 
         lax.fori_loop(0, grid_count // 8, fill, 0)
 
+        for copy in inputs[7:]:
+            copy.wait()
         box_hi, box_lo = halves(box_ref[...])
         turned = mm(box_hi, yt_ref[0]) + mm(box_lo, yt_ref[0]) + mm(box_hi, yt_ref[1])
         mid, end = PLANES * BOX, BANDS * N
@@ -337,11 +360,15 @@
         mate_pick = jnp.where(atom_base + (1 - core) * ATOMS == atoms, 1.0, 0.0).astype(BF16)
         for q in range(3):
             d_hi, d_lo = halves(d_own[:, q].reshape(half * ATOMS, N))
-            d_slot[q * N : (q + 1) * N, :] = mm(d_hi, own_pick, TN) + mm(d_lo, own_pick, TN)
+            slots = mm(d_hi, own_pick, TN) + mm(d_lo, own_pick, TN)
+            for lanes in range(2):
+                d_slot[lanes, q * N : (q + 1) * N, :] = slots[:, lanes * N : (lanes + 1) * N]
         mate.wait_recv()
         for q in range(3):
             d_hi, d_lo = halves(d_mate[:, q].reshape(half * ATOMS, N))
-            d_slot[q * N : (q + 1) * N, :] += mm(d_hi, mate_pick, TN) + mm(d_lo, mate_pick, TN)
+            slots = mm(d_hi, mate_pick, TN) + mm(d_lo, mate_pick, TN)
+            for lanes in range(2):
+                d_slot[lanes, q * N : (q + 1) * N, :] += slots[:, lanes * N : (lanes + 1) * N]
 
         for copy in atom_copies:
             copy.wait_recv()
@@ -360,14 +387,24 @@
             total += mm(c_hi, pick, NT) + mm(c_lo, pick, NT)
         summed[...] = total
 
+        d_slot[:, 3 * N :, :] = jnp.zeros((2, 24, N), F32)
+        values = [jnp.zeros((24, PAIRS), F32) for _ in range(COMBOS)]
+        for j in range(PROJ):
+            part = jnp.concatenate(
+                [
+                    jnp.concatenate(
+                        [d_slot[lanes, pl.ds(q * N + j, 8, stride=PROJ), :] for lanes in range(2)],
+                        axis=1,
+                    )
+                    for q in range(3)
+                ],
+                axis=0,
+            )
+            for combo in range(COMBOS):
+                row = j * COMBOS + combo
+                values[combo] += part * summed[row : row + 1, :]
         for combo in range(COMBOS):
-            value = jnp.zeros((PROJ, PAIRS), F32)
-            for j in range(PROJ):
-                first = (j // 7) * N + (j % 7) * PROJ
-                value += d_slot[first : first + PROJ, :] * summed[
-                    j * COMBOS + combo : j * COMBOS + combo + 1, :
-                ]
-            applied[combo, 0:PROJ, :] = value
+            applied[combo] = values[combo]
 
         depth = 32
 
@@ -377,7 +414,7 @@
             for i in range(PROJ):
                 values = proj_t[i, pl.ds(first, depth), :]
                 for combo in range(COMBOS):
-                    totals[combo] += values * applied[combo, i : i + 1, :]
+                    totals[combo] += values * applied[combo, 8 * (i // 7) + i % 7 : 8 * (i // 7) + i % 7 + 1, :]
             for combo in range(COMBOS):
                 added[pl.ds(pl.multiple_of(combo * N + first, depth), depth), :] = totals[combo]
             return carry
@@ -420,37 +457,56 @@
         q_hi, q_lo = halves(final)
         both = jnp.concatenate([q_hi, q_lo], axis=1)
 
-        def take(target):
-            picker = oh_y[target]
-            found = mm(both, jnp.concatenate([picker, picker], axis=0))
-            at = z_id == code_z[pl.ds(target, 1), :]
-            msg2[target] = jnp.concatenate(
-                [
-                    jnp.sum(
-                        jnp.where(at, found[r * BOX : (r + 1) * BOX], 0.0), axis=0, keepdims=True
+        batch = 4
+
+        def take(targets):
+            for first in range(0, batch, 2):
+                two = targets[first : first + 2]
+                pick = jnp.concatenate([oh_y[target] for target in two], axis=1)
+                found = mm(both, jnp.concatenate([pick, pick], axis=0))
+                for k, target in enumerate(two):
+                    at = z_id == code_z[target]
+                    msg2[target] = jnp.concatenate(
+                        [
+                            jnp.sum(
+                                jnp.where(
+                                    at, found[r * BOX : (r + 1) * BOX, k * N : (k + 1) * N], 0.0
+                                ),
+                                axis=0,
+                                keepdims=True,
+                            )
+                            for r in range(4)
+                        ],
+                        axis=0,
                     )
-                    for r in range(4)
-                ],
-                axis=0,
-            )
-
-        def send2(step, carry):
-            target = lax.rem(me + step, grid_count)
-            take(target)
+
+        def partners(step):
+            return [lax.rem(me + far(batch * step + k), grid_count) for k in range(batch)]
+
+        def send2(target):
             to_grid(msg2.at[target], got2.at[me], s2, r2, target).start()
-            return carry
-
-        lax.fori_loop(1, grid_count, send2, 0)
-        take(me)
+
+        def take_and_send(step, carry):
+            targets = partners(step)
+            take(targets)
+            for target in targets:
+                send2(target)
+            return carry
+
+        lax.fori_loop(0, grid_count // batch - 1, take_and_send, 0)
+        targets = partners(grid_count // batch - 1)
+        take(targets)
+        for target in targets[:-1]:
+            send2(target)
         got2[me] = msg2[me]
 
         if band_count > 1:
             settle(dens_full.at[pl.ds(0, ROWS - share)], rf)
-        dens_ref[...] = dens_full[...]
-        first_freq = col_ref[...]
+        dens_out = pltpu.make_async_copy(dens_full, dens_hbm, out_sem.at[0])
+        dens_out.start()
 
         work[...] = jnp.zeros_like(work)
-        work[0:1, 0:COLS] = first_freq.astype(F32)
+        work[0:1, 0:COLS] = col_ref[...].astype(F32)
         codes = jnp.broadcast_to(work[0:1, :], (N, N)).T.astype(jnp.int32)[0:COLS]
 
         def signed(index):
@@ -470,6 +526,10 @@
                     + kinetic * psi_ref[part, member]
                 )
 
+        out_copy = pltpu.make_async_copy(out_ref, out_hbm, out_sem.at[1])
+        out_copy.start()
+
+        dens_out.wait()
         settle(msg1.at[pl.ds(0, peers)], s1)
         settle(msg2.at[pl.ds(0, peers)], s2)
         settle(d_own.at[pl.ds(0, half - 1)], sd)
@@ -479,6 +539,7 @@
         if band_count > 1:
             settle(dens_part.at[pl.ds(0, band_count - 1)], sp)
             settle(dens_full.at[pl.ds(0, ROWS - share)], sf)
+        out_copy.wait()
 
     return kernel
 
@@ -490,10 +551,8 @@
     constants = tables(grid_count)
 
     def step(psi_g, col_index, v_local, proj_values, pair_atom, pair_row, d_matrices, occupations):
-        d_flat = d_matrices.transpose(0, 2, 1)
-        d_flat = jnp.pad(d_flat, ((0, 0), (0, 3), (0, 0))).reshape(ATOMS, 3, 7 * PROJ)
-        d_flat = jnp.pad(d_flat, ((0, 0), (0, 0), (0, N - 7 * PROJ))).transpose(1, 0, 2)
-        vmem = pl.BlockSpec(memory_space=pltpu.VMEM)
+        x_table, y_table, y_back, z_table, z_back = [jnp.asarray(t) for t in constants]
+        hbm = pl.BlockSpec(memory_space=pl.ANY)
         dma = pltpu.SemaphoreType.DMA
         out, dens = pl.pallas_call(
             make_kernel(grid_count, band_count),
@@ -501,22 +560,29 @@
                 jax.ShapeDtypeStruct(psi_g.shape, F32),
                 jax.ShapeDtypeStruct((ROWS, N), F32),
             ),
-            in_specs=[
-                vmem, vmem, vmem, pl.BlockSpec(memory_space=pl.ANY), vmem, vmem, vmem,
-                pl.BlockSpec(memory_space=pltpu.SMEM),
-            ]
-            + [vmem] * 5,
-            out_specs=(vmem, vmem),
+            in_specs=[hbm] * 12 + [pl.BlockSpec(memory_space=pltpu.SMEM)],
+            out_specs=(hbm, hbm),
             scratch_shapes=[
-                pltpu.VMEM((PAIRS, PROJ, N), F32),
+                pltpu.VMEM((2, BANDS, COLS, N), F32),
+                pltpu.VMEM((1, COLS), jnp.int32),
+                pltpu.VMEM((2, 2 * N, 2 * N), BF16),
+                pltpu.VMEM((PROJ, ATOMS, PROJ), F32),
+                pltpu.VMEM((1, PAIRS), jnp.int32),
+                pltpu.VMEM((PLANES, N, N), F32),
+                pltpu.VMEM((PROJ, PAIRS, N), F32),
+                pltpu.VMEM((1, PAIRS), jnp.int32),
+                pltpu.VMEM((2, BANDS * BOX, 2 * BANDS * N), BF16),
+                pltpu.VMEM((2, 2 * N, 2 * BOX), BF16),
+                pltpu.VMEM((2, 2 * BOX, 2 * N), BF16),
+                pltpu.VMEM((2, BANDS * N, 2 * BANDS * BOX), BF16),
+                pltpu.VMEM((2, BANDS, COLS, N), F32),
                 pltpu.VMEM((PROJ, N, PAIRS), F32),
                 pltpu.VMEM((BANDS * SLOT, 2 * N), F32),
                 pltpu.VMEM((grid_count, 4, N), F32),
                 pltpu.VMEM((grid_count, 4, N), F32),
                 pltpu.VMEM((grid_count, 4, N), F32),
                 pltpu.VMEM((grid_count, 4, N), F32),
-                pltpu.VMEM((grid_count, N), jnp.int32),
-                pltpu.VMEM((grid_count, N), jnp.int32),
+                pltpu.VMEM((grid_count, 1, N), jnp.int32),
                 pltpu.VMEM((grid_count, BANDS * BOX, N), BF16),
                 pltpu.VMEM((2 * PLANES * BOX, BANDS * BOX), F32),
                 pltpu.VMEM((COMBOS * N, ROWS), F32),
@@ -528,7 +594,7 @@
                 pltpu.VMEM((N, ROWS), F32),
                 pltpu.VMEM((half, 3, ATOMS, N), F32),
                 pltpu.VMEM((half, 3, ATOMS, N), F32),
-                pltpu.VMEM((3 * N, PAIRS), F32),
+                pltpu.VMEM((2, 3 * N + 24, N), F32),
                 pltpu.VMEM((3, ATOMS, N), F32),
                 pltpu.VMEM((PROJ * COMBOS, PAIRS), F32),
                 pltpu.VMEM((COMBOS, 24, PAIRS), F32),
@@ -538,22 +604,26 @@
                 pltpu.VMEM((band_count, ROWS // band_count, N), F32),
                 pltpu.VMEM((ROWS, N), F32),
                 pltpu.VMEM((8, N), F32),
-                dma, dma, dma, dma, dma, dma, dma, dma, dma, dma,
+                dma((12,)), dma((2,)), dma, dma((grid_count // 8,)), dma, dma, dma, dma, dma, dma,
                 dma((4,)), dma((4,)), dma((4,)), dma((4,)), dma, dma, dma, dma,
             ],
             compiler_params=pltpu.CompilerParams(
-                collective_id=0, has_side_effects=True, vmem_limit_bytes=48 << 20
+                collective_id=0, has_side_effects=True, vmem_limit_bytes=60 << 20
             ),
         )(
             psi_g,
             col_index.reshape(1, COLS),
+            x_table,
+            d_matrices.transpose(1, 0, 2),
+            pair_atom.reshape(1, PAIRS),
             v_local,
-            proj_values,
-            pair_atom.reshape(1, PAIRS),
+            proj_values.transpose(1, 0, 2),
             pair_row.reshape(1, PAIRS),
-            d_flat,
+            y_table,
+            z_table,
+            z_back,
+            y_back,
             occupations.reshape(1, BANDS),
-            *[jnp.asarray(t) for t in constants],
         )
         return out, dens.reshape(PLANES, N, N)
 

time: 62 us -> 57.6 us (0.929)
  local copies, waits for them, and re-layouts: 5.68 us -> 3.11 us
  Pallas kernels: 55.3 us -> 53.6 us
    unnamed x26 -> x2, local copies, waits for them, and re-layouts: 5.56 us -> 3.11 us
    pallas_call x1, Pallas kernels: 55.3 us -> 53.6 us  [step(): pl.pallas_call(make_kernel(grid_count, band_count), out_shape=(jax.ShapeD...]
where the time goes in v2:
time: 57.6 us; the launch traced here: 57.4 us
  Pallas kernels  53.6 us (93%)
  local copies, waits for them, and re-layouts  3.11 us (5%)
  between operations  0.64 us (1%)
    pallas_call x1, Pallas kernels, step(): pl.pallas_call(make_kernel(grid_count, band_count), out_shape=(jax.ShapeD...  53.6 us
    unnamed x2, local copies, waits for them, and re-layouts  3.11 us

profile of v2, /device:TPU:1, one launch (start us, length us, event | category | flops | bytes accessed | tf_op | source)
XLA Modules:
  0.0 57.4 jit_solution(13406698812748244088)
XLA Ops:
  0.6 53.6 %shard_map.140 = (f32[2,2,48,128]{3,2,1,0:T(8,128)}, f32[256,128]{1,0:T(8,128)}) custom-call(f32[2,2,48,128]{3,2,1,0:T(8,128)} %psi_in.1, s32[1,48]{1,0:T(1,128)} %bitcast.12, bf16[2,256,256]{2,1,0:T(8,128)(2,1)} %constant.10.clone.xt_in, f32[18,8,18]{2,1,0:T(8,128)} %bitcast.9, s32[1,256]{1,0:T(1,128)} %bitcast.10, f32[2,128,128]{2,1,0:T(8,128)} %vloc_in.1, ...), custom_call_target="tpu_custom_call" | custom-call | tf_op jit(solution)/shard_map/pallas_call | solution.py:557
  54.3 1.5 %copy.17 = f32[2,2,48,128]{3,2,1,0:T(8,128)} copy(f32[2,2,48,128]{3,2,1,0:T(8,128)} %get-tuple-element.8) | data formatting | bytes 196608
  55.8 1.6 %copy.18 = f32[2,128,128]{2,1,0:T(8,128)} copy(f32[2,128,128]{2,1,0:T(8,128)} %bitcast.8) | data formatting | bytes 262144

commit v3 on v2

--- a/solution.py
+++ b/solution.py
@@ -84,22 +84,26 @@
 def make_kernel(grid_count, band_count):
     peers = grid_count - 1
     half = grid_count // 2
+    width = 4
+    height = half // width
 
     def kernel(
         psi_in, col_in, xt_in, dmat_in, atom_in, vloc_in, proj_in, row_in, yt_in, zt_in, zb_in,
         yb_in, occ_ref,
-        out_hbm, dens_hbm,
+        got2, dens_hbm,
         psi_ref, col_ref, xt_ref, dmat_ref, atom_ref, vloc_ref, proj_buf, row_ref, yt_ref, zt_ref,
-        zb_ref, yb_ref, out_ref, proj_t, psi_pad, msg1, got1, msg2, got2, code_z, oh_y, box_ref,
+        zb_ref, yb_ref, proj_t, psi_pad, msg1, got1, msg2, code_z, oh_y, box_ref,
         field, tiles, coeff, near_coeff, near_atom, atom_col, vloc_t,
         d_own, d_mate, d_slot, d_send, summed, applied, added, h_ref,
         dens_loc, dens_part, dens_full, work,
-        in_sem, out_sem, s1, r1, s2, r2, sd, rd, sm, rm, sa, ra, sc, rc, sp, rp, sf, rf,
+        in_sem, out_sem, s1, r1, s2, r2, sd, rd, sx, rx, sm, rm, sa, ra, sc, rc, sp, rp, sf, rf,
     ):
         me = lax.axis_index("grid")
         band = lax.axis_index("band")
         core = lax.rem(me, 2)
         chip = me // 2
+        at_x = lax.rem(chip, width)
+        at_y = chip // width
 
         def to_grid(src, dst, send, recv, target):
             return pltpu.make_async_remote_copy(
@@ -120,7 +124,6 @@
             return half + (1 - 2 * (step % 2)) * ((step + 1) // 2)
 
         barrier = pltpu.get_barrier_semaphore()
-
         def greet_grid(step, carry):
             pl.semaphore_signal(
                 barrier, inc=1, device_id={"grid": lax.rem(me + step, grid_count)},
@@ -146,11 +149,13 @@
                 ]
             )
         ]
-        for copy in inputs:
+        for copy in inputs[:4]:
             copy.start()
         lax.fori_loop(1, grid_count, greet_grid, 0)
         if band_count > 1:
             lax.fori_loop(1, band_count, greet_band, 0)
+        for copy in inputs[4:]:
+            copy.start()
 
         psi_pad[...] = jnp.zeros_like(psi_pad)
         for copy in inputs[:4]:
@@ -177,19 +182,19 @@
             both = spread[8 * pair : 8 * pair + 8] + pattern
             msg1[2 * pair] = both[0:4]
             msg1[2 * pair + 1] = both[4:8]
-        own_copy = pltpu.make_async_copy(msg1.at[me], got1.at[me], r1.at[grid_count // 8 - 1])
+        own_copy = pltpu.make_async_copy(msg1.at[me], got1.at[me], r1.at[grid_count // 16 - 1])
         own_copy.start()
         d_send[...] = jnp.zeros_like(d_send)
         for i in range(PROJ):
             first = (i % 7) * PROJ
             d_send[i // 7, :, first : first + PROJ] = dmat_ref[i]
-        d_own[chip] = d_send[...]
+        d_own[at_x * height + at_y] = d_send[...]
 
         pl.semaphore_wait(barrier, peers + band_count - 1)
 
         def send1(step, carry):
             target = lax.rem(me + far(step), grid_count)
-            to_grid(msg1.at[target], got1.at[me], s1, r1.at[step // 8], target).start()
+            to_grid(msg1.at[target], got1.at[me], s1, r1.at[step // 16], target).start()
             return carry
 
         lax.fori_loop(0, peers, send1, 0)
@@ -201,12 +206,9 @@
         for copy in atom_copies:
             copy.start()
 
-        def send_d(step, carry):
-            other = lax.rem(chip + step, half)
-            to_grid(d_send, d_own.at[chip], sd, rd, 2 * other + core).start()
-            return carry
-
-        lax.fori_loop(1, half, send_d, 0)
+        for step in range(1, height):
+            other = lax.rem(at_y + step, height) * width + at_x
+            to_grid(d_send, d_own.at[at_x * height + at_y], sd, rd, 2 * other + core).start()
 
         inputs[5].wait()
         for plane in range(PLANES):
@@ -222,22 +224,24 @@
                 proj_t[i, :, part * N : (part + 1) * N] = proj_buf[i, part * N : (part + 1) * N, :].T
 
         box_ref[...] = jnp.zeros_like(box_ref)
-        row_id = iota((BANDS * BOX, N), 0)
+        row_id = iota((BANDS * BOX, N), 0).astype(F32).astype(BF16)
         z_id = iota((BOX, N), 0)
+        z_id16 = z_id.astype(F32).astype(BF16)
         sub = iota((8, N), 0)
         lane = iota((8, N), 1)
+        one, zero = jnp.ones((), BF16), jnp.zeros((), BF16)
         code_place = lane // 16 == (sub + 3) % 8
         lane = iota((1, N), 1)
         filled = lane % SLOT < COLS
         upper = lane >= SLOT
 
         def fill(step, carry):
-            group = grid_count // 8 - 1 - step
-            settle(got1.at[pl.ds(0, 8)], r1.at[group])
-            total = jnp.zeros((2 * PLANES * BOX, BANDS * BOX), F32)
-            for pair in range(4):
+            group = grid_count // 16 - 1 - step
+            settle(got1.at[pl.ds(0, 16)], r1.at[group])
+            total = jnp.zeros((BANDS * BOX, 2 * PLANES * BOX), F32)
+            for pair in range(8):
                 senders = [
-                    lax.rem(me + grid_count - far(8 * group + 2 * pair + k), grid_count)
+                    lax.rem(me + grid_count - far(16 * group + 2 * pair + k), grid_count)
                     for k in range(2)
                 ]
                 data = [got1[sender] for sender in senders]
@@ -253,29 +257,34 @@
                     at_y = jnp.where(filled, (code // N) % BOX + jnp.where(upper, BOX, 0), -1)
                     at_z = jnp.where(filled, code % BOX, -1)
                     code_z[senders[k]] = at_z
-                    picker = jnp.where(row_id == at_y, 1.0, 0.0).astype(BF16)
+                    picker = jnp.where(row_id == at_y.astype(F32).astype(BF16), one, zero)
                     oh_y[senders[k]] = picker
                     picks.append(picker)
-                    high = data[k].astype(BF16).astype(F32)
-                    rest = data[k] - high
-                    at = z_id == at_z
+                    high, rest = halves(data[k])
+                    at = z_id16 == at_z.astype(F32).astype(BF16)
                     for value, store in ((high, highs), (rest, lows)):
                         store.append(
                             jnp.concatenate(
-                                [jnp.where(at, value[r : r + 1], 0.0) for r in range(4)], axis=0
-                            ).astype(BF16)
+                                [jnp.where(at, value[r : r + 1], zero) for r in range(4)], axis=0
+                            )
                         )
                 pick = jnp.concatenate(picks, axis=1)
-                total += mm(jnp.concatenate(highs, axis=1), pick, NT)
-                total += mm(jnp.concatenate(lows, axis=1), pick, NT)
+                total += mm(pick, jnp.concatenate(highs, axis=1), NT)
+                total += mm(pick, jnp.concatenate(lows, axis=1), NT)
             box_ref[...] += total
             return carry
 
-        lax.fori_loop(0, grid_count // 8, fill, 0)
+        lax.fori_loop(0, grid_count // 16, fill, 0)
+
+        settle(d_own.at[pl.ds(0, height - 1)], rd)
+        column = pl.ds(at_x * height, height)
+        for step in range(1, width):
+            other = at_y * width + lax.rem(at_x + step, width)
+            to_grid(d_own.at[column], d_own.at[column], sx, rx, 2 * other + core).start()
 
         for copy in inputs[7:]:
             copy.wait()
-        box_hi, box_lo = halves(box_ref[...])
+        box_hi, box_lo = halves(box_ref[...].T)
         turned = mm(box_hi, yt_ref[0]) + mm(box_lo, yt_ref[0]) + mm(box_hi, yt_ref[1])
         mid, end = PLANES * BOX, BANDS * N
         part_re = turned[:mid, :end] - turned[mid:, end:]
@@ -326,35 +335,27 @@
             coeff[pl.ds(pl.multiple_of(step * 8, 8), 8), :] = jnp.concatenate(found, axis=0)
             return carry
 
-        lax.fori_loop(0, PROJ // 2, project, 0)
-        coeff_copies = [
-            to_grid(coeff, near_coeff.at[i], sc.at[i], rc.at[i], near[i]) for i in range(4)
-        ]
-        for copy in coeff_copies:
-            copy.start()
-
-        if band_count > 1:
-            settle(dens_part.at[pl.ds(0, band_count - 1)], rp)
-        mine = pl.ds(pl.multiple_of(band * share, share), share)
-        dens_part[band] = dens_loc[mine, :]
-        whole = dens_part[0]
-        for other in range(1, band_count):
-            whole += dens_part[other]
-        dens_full[mine, :] = whole
-
-        def send_full(step, carry):
-            target = lax.rem(band + step, band_count)
-            to_band(dens_full.at[mine], dens_full.at[mine], sf, rf, target).start()
-            return carry
-
-        if band_count > 1:
-            lax.fori_loop(1, band_count, send_full, 0)
-
-        settle(d_own.at[pl.ds(0, half - 1)], rd)
+        coeff_copies = []
+        for part in range(3):
+            lax.fori_loop(3 * part, 3 * part + 3, project, 0)
+            rows = pl.ds(24 * part, 24)
+            coeff_copies.append(
+                [
+                    to_grid(
+                        coeff.at[rows], near_coeff.at[i, rows], sc.at[i, part], rc.at[i, part], near[i]
+                    )
+                    for i in range(4)
+                ]
+            )
+            for copy in coeff_copies[-1]:
+                copy.start()
+
+        settle(d_own.at[pl.ds(0, half - height)], rx)
         mate = to_grid(d_own, d_mate, sm, rm, 2 * chip + 1 - core)
         mate.start()
         place = iota((half * ATOMS, PAIRS), 0)
-        atom_base = (place // ATOMS) * (2 * ATOMS) + place % ATOMS
+        slot = place // ATOMS
+        atom_base = ((slot % height) * width + slot // height) * (2 * ATOMS) + place % ATOMS
         atoms = atom_ref[...]
         own_pick = jnp.where(atom_base + core * ATOMS == atoms, 1.0, 0.0).astype(BF16)
         mate_pick = jnp.where(atom_base + (1 - core) * ATOMS == atoms, 1.0, 0.0).astype(BF16)
@@ -381,7 +382,8 @@
         pick = same(atoms)
         total = mm(c_hi, pick, NT) + mm(c_lo, pick, NT)
         for i in range(4):
-            coeff_copies[i].wait_recv()
+            for part in range(3):
+                coeff_copies[part][i].wait_recv()
             c_hi, c_lo = halves(near_coeff[i])
             pick = same(near_atom[i])
             total += mm(c_hi, pick, NT) + mm(c_lo, pick, NT)
@@ -425,6 +427,23 @@
         for combo in range(COMBOS):
             here = slice(combo * N, (combo + 1) * N)
             h_ref[here, :] = vloc_t[...] * field[here, :] + projected[here]
+
+        if band_count > 1:
+            settle(dens_part.at[pl.ds(0, band_count - 1)], rp)
+        mine = pl.ds(pl.multiple_of(band * share, share), share)
+        dens_part[band] = dens_loc[mine, :]
+        whole = dens_part[0]
+        for other in range(1, band_count):
+            whole += dens_part[other]
+        dens_full[mine, :] = whole
+
+        def send_full(step, carry):
+            target = lax.rem(band + step, band_count)
+            to_band(dens_full.at[mine], dens_full.at[mine], sf, rf, target).start()
+            return carry
+
+        if band_count > 1:
+            lax.fori_loop(1, band_count, send_full, 0)
 
         spectra = []
         for plane in range(PLANES):
@@ -457,7 +476,7 @@
         q_hi, q_lo = halves(final)
         both = jnp.concatenate([q_hi, q_lo], axis=1)
 
-        batch = 4
+        batch = 16
 
         def take(targets):
             for first in range(0, batch, 2):
@@ -498,50 +517,51 @@
         take(targets)
         for target in targets[:-1]:
             send2(target)
-        got2[me] = msg2[me]
+        own_back = pltpu.make_async_copy(msg2.at[me], got2.at[me], out_sem)
+        own_back.start()
 
         if band_count > 1:
             settle(dens_full.at[pl.ds(0, ROWS - share)], rf)
-        dens_out = pltpu.make_async_copy(dens_full, dens_hbm, out_sem.at[0])
+        dens_out = pltpu.make_async_copy(dens_full, dens_hbm, in_sem.at[0])
         dens_out.start()
-
-        work[...] = jnp.zeros_like(work)
-        work[0:1, 0:COLS] = col_ref[...].astype(F32)
-        codes = jnp.broadcast_to(work[0:1, :], (N, N)).T.astype(jnp.int32)[0:COLS]
-
-        def signed(index):
-            return jnp.where(index >= N // 2, index - N, index)
-
-        fy, fz, fx = signed(codes // N), signed(codes % N), signed(iota((COLS, N), 1))
-        kinetic = KINETIC * (fx * fx + fy * fy + fz * fz).astype(F32)
-
         settle(got2.at[pl.ds(0, peers)], r2)
-        back = got2[...].reshape(grid_count * 4, N).T
-        b_hi, b_lo = halves(back)
-        result = mm(b_hi, xt_ref[0]) + mm(b_lo, xt_ref[0]) + mm(b_hi, xt_ref[1])
-        for part in range(2):
-            for member in range(BANDS):
-                out_ref[part, member] = (
-                    result[member * SLOT : member * SLOT + COLS, part * N : (part + 1) * N]
-                    + kinetic * psi_ref[part, member]
-                )
-
-        out_copy = pltpu.make_async_copy(out_ref, out_hbm, out_sem.at[1])
-        out_copy.start()
+        own_back.wait()
 
         dens_out.wait()
         settle(msg1.at[pl.ds(0, peers)], s1)
         settle(msg2.at[pl.ds(0, peers)], s2)
-        settle(d_own.at[pl.ds(0, half - 1)], sd)
+        settle(d_own.at[pl.ds(0, height - 1)], sd)
+        settle(d_own.at[pl.ds(0, half - height)], sx)
         mate.wait_send()
-        for copy in atom_copies + coeff_copies:
-            copy.wait_send()
+        for copies in [atom_copies] + coeff_copies:
+            for copy in copies:
+                copy.wait_send()
         if band_count > 1:
             settle(dens_part.at[pl.ds(0, band_count - 1)], sp)
             settle(dens_full.at[pl.ds(0, ROWS - share)], sf)
-        out_copy.wait()
-
     return kernel
+
+
+def finish(psi_ref, col_ref, table_ref, got_ref, dens_in, out_ref, dens_ref, work):
+    back = got_ref[...].reshape(got_ref.shape[0] * 4, N).T
+    b_hi, b_lo = halves(back)
+    result = mm(b_hi, table_ref[0]) + mm(b_lo, table_ref[0]) + mm(b_hi, table_ref[1])
+    dens_ref[...] = dens_in[...]
+    work[...] = jnp.zeros_like(work)
+    work[0:1, 0:COLS] = col_ref[...].astype(F32)
+    codes = jnp.broadcast_to(work[0:1, :], (N, N)).T.astype(jnp.int32)[0:COLS]
+
+    def signed(index):
+        return jnp.where(index >= N // 2, index - N, index)
+
+    fy, fz, fx = signed(codes // N), signed(codes % N), signed(iota((COLS, N), 1))
+    kinetic = KINETIC * (fx * fx + fy * fy + fz * fz).astype(F32)
+    for part in range(2):
+        for member in range(BANDS):
+            out_ref[part, member] = (
+                result[member * SLOT : member * SLOT + COLS, part * N : (part + 1) * N]
+                + kinetic * psi_ref[part, member]
+            )
 
 
 def solution(mesh):
@@ -554,10 +574,11 @@
         x_table, y_table, y_back, z_table, z_back = [jnp.asarray(t) for t in constants]
         hbm = pl.BlockSpec(memory_space=pl.ANY)
         dma = pltpu.SemaphoreType.DMA
-        out, dens = pl.pallas_call(
+        col_row = col_index.reshape(1, COLS)
+        got, dens = pl.pallas_call(
             make_kernel(grid_count, band_count),
             out_shape=(
-                jax.ShapeDtypeStruct(psi_g.shape, F32),
+                jax.ShapeDtypeStruct((grid_count, 4, N), F32),
                 jax.ShapeDtypeStruct((ROWS, N), F32),
             ),
             in_specs=[hbm] * 12 + [pl.BlockSpec(memory_space=pltpu.SMEM)],
@@ -575,16 +596,14 @@
                 pltpu.VMEM((2, 2 * N, 2 * BOX), BF16),
                 pltpu.VMEM((2, 2 * BOX, 2 * N), BF16),
                 pltpu.VMEM((2, BANDS * N, 2 * BANDS * BOX), BF16),
-                pltpu.VMEM((2, BANDS, COLS, N), F32),
                 pltpu.VMEM((PROJ, N, PAIRS), F32),
                 pltpu.VMEM((BANDS * SLOT, 2 * N), F32),
                 pltpu.VMEM((grid_count, 4, N), F32),
                 pltpu.VMEM((grid_count, 4, N), F32),
                 pltpu.VMEM((grid_count, 4, N), F32),
-                pltpu.VMEM((grid_count, 4, N), F32),
                 pltpu.VMEM((grid_count, 1, N), jnp.int32),
                 pltpu.VMEM((grid_count, BANDS * BOX, N), BF16),
-                pltpu.VMEM((2 * PLANES * BOX, BANDS * BOX), F32),
+                pltpu.VMEM((BANDS * BOX, 2 * PLANES * BOX), F32),
                 pltpu.VMEM((COMBOS * N, ROWS), F32),
                 pltpu.VMEM((COMBOS * N, PAIRS), F32),
                 pltpu.VMEM((PROJ * COMBOS, PAIRS), F32),
@@ -604,15 +623,15 @@
                 pltpu.VMEM((band_count, ROWS // band_count, N), F32),
                 pltpu.VMEM((ROWS, N), F32),
                 pltpu.VMEM((8, N), F32),
-                dma((12,)), dma((2,)), dma, dma((grid_count // 8,)), dma, dma, dma, dma, dma, dma,
-                dma((4,)), dma((4,)), dma((4,)), dma((4,)), dma, dma, dma, dma,
+                dma((12,)), dma, dma, dma((grid_count // 16,)), dma, dma, dma, dma, dma, dma, dma, dma,
+                dma((4,)), dma((4,)), dma((4, 3)), dma((4, 3)), dma, dma, dma, dma,
             ],
             compiler_params=pltpu.CompilerParams(
                 collective_id=0, has_side_effects=True, vmem_limit_bytes=60 << 20
             ),
         )(
             psi_g,
-            col_index.reshape(1, COLS),
+            col_row,
             x_table,
             d_matrices.transpose(1, 0, 2),
             pair_atom.reshape(1, PAIRS),
@@ -625,6 +644,17 @@
             y_back,
             occupations.reshape(1, BANDS),
         )
+        out, dens = pl.pallas_call(
+            finish,
+            out_shape=(
+                jax.ShapeDtypeStruct(psi_g.shape, F32),
+                jax.ShapeDtypeStruct((ROWS, N), F32),
+            ),
+            in_specs=[pl.BlockSpec(memory_space=pltpu.VMEM)] * 5,
+            out_specs=(pl.BlockSpec(memory_space=pltpu.VMEM),) * 2,
+            scratch_shapes=[pltpu.VMEM((8, N), F32)],
+            compiler_params=pltpu.CompilerParams(vmem_limit_bytes=60 << 20),
+        )(psi_g, col_row, x_table, got, dens)
         return out, dens.reshape(PLANES, N, N)
 
     return jax.shard_map(

time: 57.6 us -> 50.5 us (0.88)
  Pallas kernels: 53.6 us -> 49.7 us
  local copies, waits for them, and re-layouts: 3.11 us -> 0 us
    pallas_call x1, Pallas kernels: 53.6 us -> 47.7 us  [step(): pl.pallas_call(make_kernel(grid_count, band_count), out_shape=(jax.ShapeD...]
    unnamed x2 -> x0, local copies, waits for them, and re-layouts: 3.11 us -> none
    pallas_call x0 -> x1, Pallas kernels: none -> 2.01 us  [step(): pl.pallas_call(finish, out_shape=(jax.ShapeDtypeStruct(psi_g.shape, F32),...]
where the time goes in v3:
time: 50.5 us; the launch traced here: 50.3 us
  Pallas kernels  49.7 us (98%)
  between operations  0.64 us (1%)
    pallas_call x1, Pallas kernels, step(): pl.pallas_call(make_kernel(grid_count, band_count), out_shape=(jax.ShapeD...  47.7 us
    pallas_call x1, Pallas kernels, step(): pl.pallas_call(finish, out_shape=(jax.ShapeDtypeStruct(psi_g.shape, F32),...  2.01 us

profile of v3, /device:TPU:1, one launch (start us, length us, event | category | flops | bytes accessed | tf_op | source)
XLA Modules:
  0.0 50.3 jit_solution(2933823725007363259)
XLA Ops:
  0.6 47.7 %shard_map.140 = (f32[64,4,128]{2,1,0:T(4,128)}, f32[256,128]{1,0:T(8,128)}) custom-call(f32[2,2,48,128]{3,2,1,0:T(8,128)} %psi_ref.1, s32[1,48]{1,0:T(1,128)} %bitcast.9, bf16[2,256,256]{2,1,0:T(8,128)(2,1)} %constant.10.clone.xt_in.table_ref, f32[18,8,18]{2,1,0:T(8,128)} %bitcast.8, s32[1,256]{1,0:T(1,128)} %bitcast.11, f32[2,128,128]{2,1,0:T(8,128)} %vloc_in.1, ...), custom_call_target="tpu_custom_call" | custom-call | tf_op jit(solution)/shard_map/pallas_call | solution.py:578
  48.3 2.0 %shard_map.141 = (f32[2,2,48,128]{3,2,1,0:T(8,128)}, f32[256,128]{1,0:T(8,128)}) custom-call(f32[2,2,48,128]{3,2,1,0:T(8,128)} %psi_ref.1, s32[1,48]{1,0:T(1,128)} %bitcast.10, bf16[2,256,256]{2,1,0:T(8,128)(2,1)} %constant.10.clone.xt_in.table_ref, f32[64,4,128]{2,1,0:T(4,128)} %get-tuple-element.6.got_ref, f32[256,128]{1,0:T(8,128)} %get-tuple-element.7.dens_in), custom_call_target="tpu_custom_call" | custom-call | tf_op jit(solution)/shard_map/pallas_call | solution.py:647

commit v4 on v3

--- a/solution.py
+++ b/solution.py
@@ -96,7 +96,7 @@
         field, tiles, coeff, near_coeff, near_atom, atom_col, vloc_t,
         d_own, d_mate, d_slot, d_send, summed, applied, added, h_ref,
         dens_loc, dens_part, dens_full, work,
-        in_sem, out_sem, s1, r1, s2, r2, sd, rd, sx, rx, sm, rm, sa, ra, sc, rc, sp, rp, sf, rf,
+        here, all_here, in_sem, out_sem, s1, r1, s2, r2, sd, rd, sx, rx, sh, rh, sm, rm, sa, ra, sc, rc, sp, rp, sf, rf,
     ):
         me = lax.axis_index("grid")
         band = lax.axis_index("band")
@@ -124,18 +124,18 @@
             return half + (1 - 2 * (step % 2)) * ((step + 1) // 2)
 
         barrier = pltpu.get_barrier_semaphore()
-        def greet_grid(step, carry):
-            pl.semaphore_signal(
-                barrier, inc=1, device_id={"grid": lax.rem(me + step, grid_count)},
-                device_id_type=MESH,
-            )
-            return carry
-
-        def greet_band(step, carry):
-            pl.semaphore_signal(
-                barrier, inc=1, device_id={"band": lax.rem(band + step, band_count)},
-                device_id_type=MESH,
-            )
+        envoy = 0
+        is_envoy = me == envoy
+
+        def greet(step, carry):
+            target = lax.rem(me + far(step), grid_count)
+
+            @pl.when(target != envoy)
+            def _():
+                pl.semaphore_signal(
+                    barrier, inc=1, device_id={"grid": target}, device_id_type=MESH
+                )
+
             return carry
 
         inputs = [
@@ -151,11 +151,60 @@
         ]
         for copy in inputs[:4]:
             copy.start()
-        lax.fori_loop(1, grid_count, greet_grid, 0)
-        if band_count > 1:
-            lax.fori_loop(1, band_count, greet_band, 0)
+        lax.fori_loop(0, peers, greet, 0, unroll=9)
         for copy in inputs[4:]:
             copy.start()
+
+        early = band < 3
+        foremost = band < 2
+        middle = band == 2
+        late = band >= 3
+        share = ROWS // band_count
+        mine = pl.ds(pl.multiple_of(band * share, share), share)
+
+        def tell_group():
+            @pl.when(is_envoy)
+            def _():
+                pl.semaphore_wait(barrier, band_count - 1)
+
+                def pass_on(step, carry):
+                    pl.semaphore_signal(
+                        all_here, inc=1, device_id={"grid": lax.rem(me + far(step), grid_count)},
+                        device_id_type=MESH,
+                    )
+                    return carry
+
+                lax.fori_loop(0, peers, pass_on, 0)
+
+        def send_parts():
+            @pl.when(jnp.logical_not(is_envoy))
+            def _():
+                pl.semaphore_wait(all_here, 1)
+
+            def send_part(step, carry):
+                target = lax.rem(band + step, band_count)
+                first = pl.multiple_of(target * share, share)
+                to_band(
+                    dens_loc.at[pl.ds(first, share)], dens_part.at[band], sp, rp, target
+                ).start()
+                return carry
+
+            lax.fori_loop(1, band_count, send_part, 0)
+
+        def add_parts():
+            settle(dens_part.at[pl.ds(0, band_count - 1)], rp)
+            dens_part[band] = dens_loc[mine, :]
+            whole = dens_part[0]
+            for other in range(1, band_count):
+                whole += dens_part[other]
+            dens_full[mine, :] = whole
+
+            def send_full(step, carry):
+                target = lax.rem(band + step, band_count)
+                to_band(dens_full.at[mine], dens_full.at[mine], sf, rf, target).start()
+                return carry
+
+            lax.fori_loop(1, band_count, send_full, 0)
 
         psi_pad[...] = jnp.zeros_like(psi_pad)
         for copy in inputs[:4]:
@@ -190,14 +239,32 @@
             d_send[i // 7, :, first : first + PROJ] = dmat_ref[i]
         d_own[at_x * height + at_y] = d_send[...]
 
-        pl.semaphore_wait(barrier, peers + band_count - 1)
-
-        def send1(step, carry):
+        @pl.when(jnp.logical_not(is_envoy))
+        def _():
+            pl.semaphore_wait(barrier, peers)
+            pl.semaphore_signal(here, inc=1, device_id={"grid": envoy}, device_id_type=MESH)
+
+        @pl.when(is_envoy)
+        def _():
+            pl.semaphore_wait(here, peers)
+
+        def send1(count, carry):
+            step = peers - 1 - count
             target = lax.rem(me + far(step), grid_count)
             to_grid(msg1.at[target], got1.at[me], s1, r1.at[step // 16], target).start()
             return carry
 
-        lax.fori_loop(0, peers, send1, 0)
+        lax.fori_loop(0, peers, send1, 0, unroll=9)
+        if band_count > 1:
+
+            @pl.when(is_envoy)
+            def _():
+                for step in range(1, band_count):
+                    pl.semaphore_signal(
+                        barrier, inc=1, device_id={"band": lax.rem(band + step, band_count)},
+                        device_id_type=MESH,
+                    )
+
         near = [lax.rem(me + off + grid_count, grid_count) for off in (1, -1, 2, -2)]
         inputs[4].wait()
         atom_copies = [
@@ -235,9 +302,17 @@
         filled = lane % SLOT < COLS
         upper = lane >= SLOT
 
+        apart = lax.rem(me - envoy + grid_count, grid_count)
+        envoy_step = jnp.where(apart > half, 2 * (apart - half), 2 * (half - apart) - 1)
+        last_group = jnp.where(apart == half, 0, envoy_step // 16)
+        groups = grid_count // 16
+
         def fill(step, carry):
-            group = grid_count // 16 - 1 - step
-            settle(got1.at[pl.ds(0, 16)], r1.at[group])
+            group = groups - 1 - step
+            group = jnp.where(group > last_group, group, group - 1)
+            group = jnp.where(step == groups - 1, last_group, group)
+            with jax.named_scope("s_fillwait"):
+                settle(got1.at[pl.ds(0, 16)], r1.at[group])
             total = jnp.zeros((BANDS * BOX, 2 * PLANES * BOX), F32)
             for pair in range(8):
                 senders = [
@@ -274,14 +349,28 @@
             box_ref[...] += total
             return carry
 
-        lax.fori_loop(0, grid_count // 16, fill, 0)
-
+        lax.fori_loop(0, groups - 1, fill, 0)
         settle(d_own.at[pl.ds(0, height - 1)], rd)
-        column = pl.ds(at_x * height, height)
-        for step in range(1, width):
-            other = at_y * width + lax.rem(at_x + step, width)
-            to_grid(d_own.at[column], d_own.at[column], sx, rx, 2 * other + core).start()
-
+
+        def column(offset, first=0, count=height):
+            return pl.ds(lax.rem(at_x + offset + width, width) * height + first, count)
+
+        def along_x(offset):
+            return 2 * (at_y * width + lax.rem(at_x + offset + width, width)) + core
+
+        def to_mate(block):
+            to_grid(d_own.at[block], d_mate.at[block], sm, rm, 2 * chip + 1 - core).start()
+
+        for offset in (1, -1):
+            block = d_own.at[column(0)]
+            to_grid(block, block, sx, rx, along_x(offset)).start()
+        if band_count > 1:
+
+            @pl.when(jnp.logical_not(early))
+            def _():
+                tell_group()
+
+        lax.fori_loop(groups - 1, groups, fill, 0)
         for copy in inputs[7:]:
             copy.wait()
         box_hi, box_lo = halves(box_ref[...].T)
@@ -301,6 +390,13 @@
                         part * N : (part + 1) * N, member * N : (member + 1) * N
                     ]
 
+        settle(d_own.at[pl.ds(0, 2 * height)], rx)
+        for offset, first in ((1, 0), (-1, height // 2)):
+            block = d_own.at[column(-offset, first, height // 2)]
+            to_grid(block, block, sh, rh, along_x(offset)).start()
+        for offset in (0, 1, -1):
+            to_mate(column(offset))
+
         dens_t = jnp.zeros((N, ROWS), F32)
         for member in range(BANDS):
             real = field[member * N : (member + 1) * N, :]
@@ -308,16 +404,16 @@
             dens_t += occ_ref[0, member] * (real * real + imag * imag)
         for plane in range(PLANES):
             dens_loc[plane * N : (plane + 1) * N, :] = dens_t[:, plane * N : (plane + 1) * N].T
-        share = ROWS // band_count
-
-        def send_part(step, carry):
-            target = lax.rem(band + step, band_count)
-            first = pl.multiple_of(target * share, share)
-            to_band(dens_loc.at[pl.ds(first, share)], dens_part.at[band], sp, rp, target).start()
-            return carry
 
         if band_count > 1:
-            lax.fori_loop(1, band_count, send_part, 0)
+
+            @pl.when(early)
+            def _():
+                tell_group()
+
+            @pl.when(jnp.logical_not(early))
+            def _():
+                send_parts()
 
         local_row = row_ref[...] - me * ROWS
         row_pick = jnp.where(iota((ROWS, PAIRS), 0) == local_row, 1.0, 0.0).astype(BF16)
@@ -350,9 +446,14 @@
             for copy in coeff_copies[-1]:
                 copy.start()
 
-        settle(d_own.at[pl.ds(0, half - height)], rx)
-        mate = to_grid(d_own, d_mate, sm, rm, 2 * chip + 1 - core)
-        mate.start()
+        if band_count > 1:
+
+            @pl.when(early)
+            def _():
+                send_parts()
+
+        settle(d_own.at[pl.ds(0, height)], rh)
+        to_mate(column(2))
         place = iota((half * ATOMS, PAIRS), 0)
         slot = place // ATOMS
         atom_base = ((slot % height) * width + slot // height) * (2 * ATOMS) + place % ATOMS
@@ -364,13 +465,19 @@
             slots = mm(d_hi, own_pick, TN) + mm(d_lo, own_pick, TN)
             for lanes in range(2):
                 d_slot[lanes, q * N : (q + 1) * N, :] = slots[:, lanes * N : (lanes + 1) * N]
-        mate.wait_recv()
+        settle(d_mate, rm)
         for q in range(3):
             d_hi, d_lo = halves(d_mate[:, q].reshape(half * ATOMS, N))
             slots = mm(d_hi, mate_pick, TN) + mm(d_lo, mate_pick, TN)
             for lanes in range(2):
                 d_slot[lanes, q * N : (q + 1) * N, :] += slots[:, lanes * N : (lanes + 1) * N]
 
+        if band_count > 1:
+
+            @pl.when(late)
+            def _():
+                add_parts()
+
         for copy in atom_copies:
             copy.wait_recv()
         column = jnp.concatenate([atom_col[...], atom_col[...]], axis=1)
@@ -382,8 +489,9 @@
         pick = same(atoms)
         total = mm(c_hi, pick, NT) + mm(c_lo, pick, NT)
         for i in range(4):
-            for part in range(3):
-                coeff_copies[part][i].wait_recv()
+            with jax.named_scope("s_coefwait"):
+                for part in range(3):
+                    coeff_copies[part][i].wait_recv()
             c_hi, c_lo = halves(near_coeff[i])
             pick = same(near_atom[i])
             total += mm(c_hi, pick, NT) + mm(c_lo, pick, NT)
@@ -427,23 +535,6 @@
         for combo in range(COMBOS):
             here = slice(combo * N, (combo + 1) * N)
             h_ref[here, :] = vloc_t[...] * field[here, :] + projected[here]
-
-        if band_count > 1:
-            settle(dens_part.at[pl.ds(0, band_count - 1)], rp)
-        mine = pl.ds(pl.multiple_of(band * share, share), share)
-        dens_part[band] = dens_loc[mine, :]
-        whole = dens_part[0]
-        for other in range(1, band_count):
-            whole += dens_part[other]
-        dens_full[mine, :] = whole
-
-        def send_full(step, carry):
-            target = lax.rem(band + step, band_count)
-            to_band(dens_full.at[mine], dens_full.at[mine], sf, rf, target).start()
-            return carry
-
-        if band_count > 1:
-            lax.fori_loop(1, band_count, send_full, 0)
 
         spectra = []
         for plane in range(PLANES):
@@ -476,6 +567,12 @@
         q_hi, q_lo = halves(final)
         both = jnp.concatenate([q_hi, q_lo], axis=1)
 
+        if band_count > 1:
+
+            @pl.when(middle)
+            def _():
+                add_parts()
+
         batch = 16
 
         def take(targets):
@@ -521,6 +618,11 @@
         own_back.start()
 
         if band_count > 1:
+
+            @pl.when(foremost)
+            def _():
+                add_parts()
+
             settle(dens_full.at[pl.ds(0, ROWS - share)], rf)
         dens_out = pltpu.make_async_copy(dens_full, dens_hbm, in_sem.at[0])
         dens_out.start()
@@ -531,8 +633,9 @@
         settle(msg1.at[pl.ds(0, peers)], s1)
         settle(msg2.at[pl.ds(0, peers)], s2)
         settle(d_own.at[pl.ds(0, height - 1)], sd)
-        settle(d_own.at[pl.ds(0, half - height)], sx)
-        mate.wait_send()
+        settle(d_own.at[pl.ds(0, 2 * height)], sx)
+        settle(d_own.at[pl.ds(0, height)], sh)
+        settle(d_mate, sm)
         for copies in [atom_copies] + coeff_copies:
             for copy in copies:
                 copy.wait_send()
@@ -623,7 +726,8 @@
                 pltpu.VMEM((band_count, ROWS // band_count, N), F32),
                 pltpu.VMEM((ROWS, N), F32),
                 pltpu.VMEM((8, N), F32),
-                dma((12,)), dma, dma, dma((grid_count // 16,)), dma, dma, dma, dma, dma, dma, dma, dma,
+                pltpu.SemaphoreType.REGULAR, pltpu.SemaphoreType.REGULAR,
+                dma((12,)), dma, dma, dma((grid_count // 16,)), dma, dma, dma, dma, dma, dma, dma, dma, dma, dma,
                 dma((4,)), dma((4,)), dma((4, 3)), dma((4, 3)), dma, dma, dma, dma,
             ],
             compiler_params=pltpu.CompilerParams(

time: 50.5 us -> 45.8 us (0.907); the launches traced: 50.3 us -> 44.9 us
  Pallas kernels: 49.7 us -> 44.2 us
    pallas_call x1, Pallas kernels: 47.7 us -> 42.2 us  [step(): pl.pallas_call(make_kernel(grid_count, band_count), out_shape=(jax.ShapeD...]
where the time goes in v4:
time: 45.8 us; the launch traced here: 44.9 us
  Pallas kernels  44.2 us (97%)
  between operations  0.64 us (1%)
    pallas_call x1, Pallas kernels, step(): pl.pallas_call(make_kernel(grid_count, band_count), out_shape=(jax.ShapeD...  42.2 us
    pallas_call x1, Pallas kernels, step(): pl.pallas_call(finish, out_shape=(jax.ShapeDtypeStruct(psi_g.shape, F32),...  2.01 us

profile of v4, /device:TPU:1, one launch (start us, length us, event | category | flops | bytes accessed | tf_op | source)
XLA Modules:
  0.0 44.9 jit_solution(7988117443987251628)
XLA Ops:
  0.6 42.2 %shard_map.140 = (f32[64,4,128]{2,1,0:T(4,128)}, f32[256,128]{1,0:T(8,128)}) custom-call(f32[2,2,48,128]{3,2,1,0:T(8,128)} %psi_ref.1, s32[1,48]{1,0:T(1,128)} %bitcast.9, bf16[2,256,256]{2,1,0:T(8,128)(2,1)} %constant.10.clone.xt_in.table_ref, f32[18,8,18]{2,1,0:T(8,128)} %bitcast.8, s32[1,256]{1,0:T(1,128)} %bitcast.11, f32[2,128,128]{2,1,0:T(8,128)} %vloc_in.1, ...), custom_call_target="tpu_custom_call" | custom-call | tf_op jit(solution)/shard_map/pallas_call | solution.py:681
  42.9 2.0 %shard_map.141 = (f32[2,2,48,128]{3,2,1,0:T(8,128)}, f32[256,128]{1,0:T(8,128)}) custom-call(f32[2,2,48,128]{3,2,1,0:T(8,128)} %psi_ref.1, s32[1,48]{1,0:T(1,128)} %bitcast.10, bf16[2,256,256]{2,1,0:T(8,128)(2,1)} %constant.10.clone.xt_in.table_ref, f32[64,4,128]{2,1,0:T(4,128)} %get-tuple-element.6.got_ref, f32[256,128]{1,0:T(8,128)} %get-tuple-element.7.dens_in), custom_call_target="tpu_custom_call" | custom-call | tf_op jit(solution)/shard_map/pallas_call | solution.py:751

commit v5 on v4

--- a/solution.py
+++ b/solution.py
@@ -95,8 +95,8 @@
         zb_ref, yb_ref, proj_t, psi_pad, msg1, got1, msg2, code_z, oh_y, box_ref,
         field, tiles, coeff, near_coeff, near_atom, atom_col, vloc_t,
         d_own, d_mate, d_slot, d_send, summed, applied, added, h_ref,
-        dens_loc, dens_part, dens_full, work,
-        here, all_here, in_sem, out_sem, s1, r1, s2, r2, sd, rd, sx, rx, sh, rh, sm, rm, sa, ra, sc, rc, sp, rp, sf, rf,
+        dens_loc, dens_part, dens_full, work, row_pick, d_pick, same,
+        here, all_here, in_sem, out_sem, s1, r1, s2, r2, sd, rd, sx, rx, sm, rm, sa, ra, sc, rc, sp, rp, sf, rf,
     ):
         me = lax.axis_index("grid")
         band = lax.axis_index("band")
@@ -126,6 +126,11 @@
         barrier = pltpu.get_barrier_semaphore()
         envoy = 0
         is_envoy = me == envoy
+
+        apart = lax.rem(me - envoy + grid_count, grid_count)
+        envoy_step = jnp.where(apart > half, 2 * (apart - half), 2 * (half - apart) - 1)
+        last_group = jnp.where(apart == half, 0, envoy_step // 16)
+        groups = grid_count // 16
 
         def greet(step, carry):
             target = lax.rem(me + far(step), grid_count)
@@ -242,11 +247,9 @@
         @pl.when(jnp.logical_not(is_envoy))
         def _():
             pl.semaphore_wait(barrier, peers)
-            pl.semaphore_signal(here, inc=1, device_id={"grid": envoy}, device_id_type=MESH)
-
-        @pl.when(is_envoy)
-        def _():
-            pl.semaphore_wait(here, peers)
+            pl.semaphore_signal(
+                here.at[last_group], inc=1, device_id={"grid": envoy}, device_id_type=MESH
+            )
 
         def send1(count, carry):
             step = peers - 1 - count
@@ -254,7 +257,17 @@
             to_grid(msg1.at[target], got1.at[me], s1, r1.at[step // 16], target).start()
             return carry
 
-        lax.fori_loop(0, peers, send1, 0, unroll=9)
+        @pl.when(jnp.logical_not(is_envoy))
+        def _():
+            lax.fori_loop(0, peers, send1, 0, unroll=9)
+
+        @pl.when(is_envoy)
+        def _():
+            for group in range(groups):
+                sent = max(16 * group - 1, 0)
+                pl.semaphore_wait(here.at[groups - 1 - group], 16 * group + 15 - sent)
+                lax.fori_loop(sent, 16 * group + 15, send1, 0)
+
         if band_count > 1:
 
             @pl.when(is_envoy)
@@ -285,10 +298,26 @@
             atom_col[part * N : (part + 1) * N, :] = jnp.broadcast_to(
                 atom_row[:, part * N : (part + 1) * N], (N, N)
             ).T
-        inputs[6].wait()
+        for copy in inputs[6:]:
+            copy.wait()
         for i in range(PROJ):
             for part in range(2):
                 proj_t[i, :, part * N : (part + 1) * N] = proj_buf[i, part * N : (part + 1) * N, :].T
+
+        local_row = row_ref[...] - me * ROWS
+        row_pick[...] = jnp.where(iota((ROWS, PAIRS), 0) == local_row, 1.0, 0.0).astype(BF16)
+        atoms = atom_ref[...]
+        place = iota((half * ATOMS, PAIRS), 0)
+        slot = place // ATOMS
+        atom_base = ((slot % height) * width + slot // height) * (2 * ATOMS) + place % ATOMS
+        for which in range(2):
+            shift = jnp.where(which == 0, core, 1 - core) * ATOMS
+            d_pick[which] = jnp.where(atom_base + shift == atoms, 1.0, 0.0).astype(BF16)
+        wide = jnp.concatenate([atom_col[...], atom_col[...]], axis=1)
+        same[0] = jnp.where(wide == atom_row, 1.0, 0.0).astype(BF16)
+        for i in range(4):
+            atom_copies[i].wait_recv()
+            same[1 + i] = jnp.where(wide == near_atom[i].astype(F32), 1.0, 0.0).astype(BF16)
 
         box_ref[...] = jnp.zeros_like(box_ref)
         row_id = iota((BANDS * BOX, N), 0).astype(F32).astype(BF16)
@@ -301,11 +330,6 @@
         lane = iota((1, N), 1)
         filled = lane % SLOT < COLS
         upper = lane >= SLOT
-
-        apart = lax.rem(me - envoy + grid_count, grid_count)
-        envoy_step = jnp.where(apart > half, 2 * (apart - half), 2 * (half - apart) - 1)
-        last_group = jnp.where(apart == half, 0, envoy_step // 16)
-        groups = grid_count // 16
 
         def fill(step, carry):
             group = groups - 1 - step
@@ -349,30 +373,30 @@
             box_ref[...] += total
             return carry
 
-        lax.fori_loop(0, groups - 1, fill, 0)
+        lax.fori_loop(0, groups // 2, fill, 0)
+        if band_count > 1:
+
+            @pl.when(jnp.logical_not(early))
+            def _():
+                tell_group()
+
+        lax.fori_loop(groups // 2, groups - 1, fill, 0)
         settle(d_own.at[pl.ds(0, height - 1)], rd)
 
-        def column(offset, first=0, count=height):
-            return pl.ds(lax.rem(at_x + offset + width, width) * height + first, count)
-
-        def along_x(offset):
-            return 2 * (at_y * width + lax.rem(at_x + offset + width, width)) + core
+        def column(offset):
+            return pl.ds(lax.rem(at_x + offset + width, width) * height, height)
+
+        for i, offset in enumerate((2, 1, -1)):
+            block = d_own.at[column(0)]
+            target = 2 * (at_y * width + lax.rem(at_x + offset + width, width)) + core
+            to_grid(block, block, sx.at[i], rx.at[i], target).start()
 
         def to_mate(block):
             to_grid(d_own.at[block], d_mate.at[block], sm, rm, 2 * chip + 1 - core).start()
 
-        for offset in (1, -1):
-            block = d_own.at[column(0)]
-            to_grid(block, block, sx, rx, along_x(offset)).start()
-        if band_count > 1:
-
-            @pl.when(jnp.logical_not(early))
-            def _():
-                tell_group()
-
+        to_mate(column(0))
         lax.fori_loop(groups - 1, groups, fill, 0)
-        for copy in inputs[7:]:
-            copy.wait()
+
         box_hi, box_lo = halves(box_ref[...].T)
         turned = mm(box_hi, yt_ref[0]) + mm(box_lo, yt_ref[0]) + mm(box_hi, yt_ref[1])
         mid, end = PLANES * BOX, BANDS * N
@@ -390,13 +414,6 @@
                         part * N : (part + 1) * N, member * N : (member + 1) * N
                     ]
 
-        settle(d_own.at[pl.ds(0, 2 * height)], rx)
-        for offset, first in ((1, 0), (-1, height // 2)):
-            block = d_own.at[column(-offset, first, height // 2)]
-            to_grid(block, block, sh, rh, along_x(offset)).start()
-        for offset in (0, 1, -1):
-            to_mate(column(offset))
-
         dens_t = jnp.zeros((N, ROWS), F32)
         for member in range(BANDS):
             real = field[member * N : (member + 1) * N, :]
@@ -415,10 +432,8 @@
             def _():
                 send_parts()
 
-        local_row = row_ref[...] - me * ROWS
-        row_pick = jnp.where(iota((ROWS, PAIRS), 0) == local_row, 1.0, 0.0).astype(BF16)
         f_hi, f_lo = halves(field[...])
-        tiles[...] = mm(f_hi, row_pick) + mm(f_lo, row_pick)
+        tiles[...] = mm(f_hi, row_pick[...]) + mm(f_lo, row_pick[...])
 
         def project(step, carry):
             found = []
@@ -452,23 +467,18 @@
             def _():
                 send_parts()
 
-        settle(d_own.at[pl.ds(0, height)], rh)
-        to_mate(column(2))
-        place = iota((half * ATOMS, PAIRS), 0)
-        slot = place // ATOMS
-        atom_base = ((slot % height) * width + slot // height) * (2 * ATOMS) + place % ATOMS
-        atoms = atom_ref[...]
-        own_pick = jnp.where(atom_base + core * ATOMS == atoms, 1.0, 0.0).astype(BF16)
-        mate_pick = jnp.where(atom_base + (1 - core) * ATOMS == atoms, 1.0, 0.0).astype(BF16)
+        for i, offset in ((1, 1), (2, -1), (0, 2)):
+            settle(d_own.at[pl.ds(0, height)], rx.at[i])
+            to_mate(column(-offset))
         for q in range(3):
             d_hi, d_lo = halves(d_own[:, q].reshape(half * ATOMS, N))
-            slots = mm(d_hi, own_pick, TN) + mm(d_lo, own_pick, TN)
+            slots = mm(d_hi, d_pick[0], TN) + mm(d_lo, d_pick[0], TN)
             for lanes in range(2):
                 d_slot[lanes, q * N : (q + 1) * N, :] = slots[:, lanes * N : (lanes + 1) * N]
         settle(d_mate, rm)
         for q in range(3):
             d_hi, d_lo = halves(d_mate[:, q].reshape(half * ATOMS, N))
-            slots = mm(d_hi, mate_pick, TN) + mm(d_lo, mate_pick, TN)
+            slots = mm(d_hi, d_pick[1], TN) + mm(d_lo, d_pick[1], TN)
             for lanes in range(2):
                 d_slot[lanes, q * N : (q + 1) * N, :] += slots[:, lanes * N : (lanes + 1) * N]
 
@@ -478,23 +488,14 @@
             def _():
                 add_parts()
 
-        for copy in atom_copies:
-            copy.wait_recv()
-        column = jnp.concatenate([atom_col[...], atom_col[...]], axis=1)
-
-        def same(other_row):
-            return jnp.where(column == other_row.astype(F32), 1.0, 0.0).astype(BF16)
-
         c_hi, c_lo = halves(coeff[...])
-        pick = same(atoms)
-        total = mm(c_hi, pick, NT) + mm(c_lo, pick, NT)
+        total = mm(c_hi, same[0], NT) + mm(c_lo, same[0], NT)
         for i in range(4):
             with jax.named_scope("s_coefwait"):
                 for part in range(3):
                     coeff_copies[part][i].wait_recv()
             c_hi, c_lo = halves(near_coeff[i])
-            pick = same(near_atom[i])
-            total += mm(c_hi, pick, NT) + mm(c_lo, pick, NT)
+            total += mm(c_hi, same[1 + i], NT) + mm(c_lo, same[1 + i], NT)
         summed[...] = total
 
         d_slot[:, 3 * N :, :] = jnp.zeros((2, 24, N), F32)
@@ -531,7 +532,7 @@
 
         lax.fori_loop(0, N // depth, spread_back, 0)
         a_hi, a_lo = halves(added[...])
-        projected = mm(a_hi, row_pick, NT) + mm(a_lo, row_pick, NT)
+        projected = mm(a_hi, row_pick[...], NT) + mm(a_lo, row_pick[...], NT)
         for combo in range(COMBOS):
             here = slice(combo * N, (combo + 1) * N)
             h_ref[here, :] = vloc_t[...] * field[here, :] + projected[here]
@@ -633,8 +634,8 @@
         settle(msg1.at[pl.ds(0, peers)], s1)
         settle(msg2.at[pl.ds(0, peers)], s2)
         settle(d_own.at[pl.ds(0, height - 1)], sd)
-        settle(d_own.at[pl.ds(0, 2 * height)], sx)
-        settle(d_own.at[pl.ds(0, height)], sh)
+        for i in range(3):
+            settle(d_own.at[pl.ds(0, height)], sx.at[i])
         settle(d_mate, sm)
         for copies in [atom_copies] + coeff_copies:
             for copy in copies:
@@ -726,8 +727,11 @@
                 pltpu.VMEM((band_count, ROWS // band_count, N), F32),
                 pltpu.VMEM((ROWS, N), F32),
                 pltpu.VMEM((8, N), F32),
-                pltpu.SemaphoreType.REGULAR, pltpu.SemaphoreType.REGULAR,
-                dma((12,)), dma, dma, dma((grid_count // 16,)), dma, dma, dma, dma, dma, dma, dma, dma, dma, dma,
+                pltpu.VMEM((ROWS, PAIRS), BF16),
+                pltpu.VMEM((2, half * ATOMS, PAIRS), BF16),
+                pltpu.VMEM((5, PAIRS, PAIRS), BF16),
+                pltpu.SemaphoreType.REGULAR((grid_count // 16,)), pltpu.SemaphoreType.REGULAR,
+                dma((12,)), dma, dma, dma((grid_count // 16,)), dma, dma, dma, dma, dma((3,)), dma((3,)), dma, dma,
                 dma((4,)), dma((4,)), dma((4, 3)), dma((4, 3)), dma, dma, dma, dma,
             ],
             compiler_params=pltpu.CompilerParams(

time: 45.8 us -> 46 us (level)
  the two profiles are of different devices: /device:TPU:1 before, /device:TPU:9 now
where the time goes in v5:
time: 46 us; the launch traced here: 45.9 us
  Pallas kernels  45.2 us (98%)
  between operations  0.64 us (1%)
    pallas_call x1, Pallas kernels, step(): pl.pallas_call(make_kernel(grid_count, band_count), out_shape=(jax.ShapeD...  43.2 us
    pallas_call x1, Pallas kernels, step(): pl.pallas_call(finish, out_shape=(jax.ShapeDtypeStruct(psi_g.shape, F32),...  2.01 us

profile of v5, /device:TPU:9, one launch (start us, length us, event | category | flops | bytes accessed | tf_op | source)
XLA Modules:
  0.0 45.9 jit_solution(16311266646180831334)
XLA Ops:
  0.6 43.2 %shard_map.140 = (f32[64,4,128]{2,1,0:T(4,128)}, f32[256,128]{1,0:T(8,128)}) custom-call(f32[2,2,48,128]{3,2,1,0:T(8,128)} %psi_ref.1, s32[1,48]{1,0:T(1,128)} %bitcast.9, bf16[2,256,256]{2,1,0:T(8,128)(2,1)} %constant.10.clone.xt_in.table_ref, f32[18,8,18]{2,1,0:T(8,128)} %bitcast.8, s32[1,256]{1,0:T(1,128)} %bitcast.11, f32[2,128,128]{2,1,0:T(8,128)} %vloc_in.1, ...), custom_call_target="tpu_custom_call" | custom-call | tf_op jit(solution)/shard_map/pallas_call | solution.py:682
  43.9 2.0 %shard_map.141 = (f32[2,2,48,128]{3,2,1,0:T(8,128)}, f32[256,128]{1,0:T(8,128)}) custom-call(f32[2,2,48,128]{3,2,1,0:T(8,128)} %psi_ref.1, s32[1,48]{1,0:T(1,128)} %bitcast.10, bf16[2,256,256]{2,1,0:T(8,128)(2,1)} %constant.10.clone.xt_in.table_ref, f32[64,4,128]{2,1,0:T(4,128)} %get-tuple-element.6.got_ref, f32[256,128]{1,0:T(8,128)} %get-tuple-element.7.dens_in), custom_call_target="tpu_custom_call" | custom-call | tf_op jit(solution)/shard_map/pallas_call | solution.py:755

commit v6 on v5

--- a/solution.py
+++ b/solution.py
@@ -94,9 +94,9 @@
         psi_ref, col_ref, xt_ref, dmat_ref, atom_ref, vloc_ref, proj_buf, row_ref, yt_ref, zt_ref,
         zb_ref, yb_ref, proj_t, psi_pad, msg1, got1, msg2, code_z, oh_y, box_ref,
         field, tiles, coeff, near_coeff, near_atom, atom_col, vloc_t,
-        d_own, d_mate, d_slot, d_send, summed, applied, added, h_ref,
+        d_own, d_mate, d_rest, rest_mate, d_slot, d_send, summed, applied, added, h_ref,
         dens_loc, dens_part, dens_full, work, row_pick, d_pick, same,
-        here, all_here, in_sem, out_sem, s1, r1, s2, r2, sd, rd, sx, rx, sm, rm, sa, ra, sc, rc, sp, rp, sf, rf,
+        here, all_here, in_sem, out_sem, s1, r1, s2, r2, sd, rd, sx, rx, se, re, sg, rg, sh, rh, sm, rm, sa, ra, sc, rc, sp, rp, sf, rf,
     ):
         me = lax.axis_index("grid")
         band = lax.axis_index("band")
@@ -120,28 +120,29 @@
         def settle(ref, sem):
             pltpu.make_async_copy(ref, ref, sem).wait()
 
-        def far(step):
-            return half + (1 - 2 * (step % 2)) * ((step + 1) // 2)
+        def wrap(index):
+            return jnp.where(index >= grid_count, index - grid_count, index)
+
+        def far(pair):
+            return half + pair, half - 1 - pair
 
         barrier = pltpu.get_barrier_semaphore()
         envoy = 0
         is_envoy = me == envoy
 
-        apart = lax.rem(me - envoy + grid_count, grid_count)
+        apart = wrap(me - envoy + grid_count)
         envoy_step = jnp.where(apart > half, 2 * (apart - half), 2 * (half - apart) - 1)
         last_group = jnp.where(apart == half, 0, envoy_step // 16)
         groups = grid_count // 16
 
-        def greet(step, carry):
-            target = lax.rem(me + far(step), grid_count)
+        def greet(offset):
+            target = wrap(me + offset)
 
             @pl.when(target != envoy)
             def _():
                 pl.semaphore_signal(
                     barrier, inc=1, device_id={"grid": target}, device_id_type=MESH
                 )
-
-            return carry
 
         inputs = [
             pltpu.make_async_copy(src, dst, in_sem.at[i])
@@ -156,14 +157,17 @@
         ]
         for copy in inputs[:4]:
             copy.start()
-        lax.fori_loop(0, peers, greet, 0, unroll=9)
+        for pair in range(half):
+            for offset in far(pair):
+                if offset > 0:
+                    greet(offset)
         for copy in inputs[4:]:
             copy.start()
 
         early = band < 3
-        foremost = band < 2
-        middle = band == 2
-        late = band >= 3
+        foremost = band < 3
+        middle = band == 3
+        late = band >= 4
         share = ROWS // band_count
         mine = pl.ds(pl.multiple_of(band * share, share), share)
 
@@ -172,14 +176,13 @@
             def _():
                 pl.semaphore_wait(barrier, band_count - 1)
 
-                def pass_on(step, carry):
+                def pass_on(offset, carry):
                     pl.semaphore_signal(
-                        all_here, inc=1, device_id={"grid": lax.rem(me + far(step), grid_count)},
-                        device_id_type=MESH,
+                        all_here, inc=1, device_id={"grid": wrap(me + offset)}, device_id_type=MESH
                     )
                     return carry
 
-                lax.fori_loop(0, peers, pass_on, 0)
+                lax.fori_loop(1, grid_count, pass_on, 0)
 
         def send_parts():
             @pl.when(jnp.logical_not(is_envoy))
@@ -187,14 +190,14 @@
                 pl.semaphore_wait(all_here, 1)
 
             def send_part(step, carry):
-                target = lax.rem(band + step, band_count)
+                target = jnp.where(step >= band, step + 1, step)
                 first = pl.multiple_of(target * share, share)
                 to_band(
                     dens_loc.at[pl.ds(first, share)], dens_part.at[band], sp, rp, target
                 ).start()
                 return carry
 
-            lax.fori_loop(1, band_count, send_part, 0)
+            lax.fori_loop(0, band_count - 1, send_part, 0)
 
         def add_parts():
             settle(dens_part.at[pl.ds(0, band_count - 1)], rp)
@@ -205,14 +208,14 @@
             dens_full[mine, :] = whole
 
             def send_full(step, carry):
-                target = lax.rem(band + step, band_count)
+                target = jnp.where(step >= band, step + 1, step)
                 to_band(dens_full.at[mine], dens_full.at[mine], sf, rf, target).start()
                 return carry
 
-            lax.fori_loop(1, band_count, send_full, 0)
+            lax.fori_loop(0, band_count - 1, send_full, 0)
 
         psi_pad[...] = jnp.zeros_like(psi_pad)
-        for copy in inputs[:4]:
+        for copy in inputs[:3]:
             copy.wait()
         for member in range(BANDS):
             for part in range(2):
@@ -238,11 +241,6 @@
             msg1[2 * pair + 1] = both[4:8]
         own_copy = pltpu.make_async_copy(msg1.at[me], got1.at[me], r1.at[grid_count // 16 - 1])
         own_copy.start()
-        d_send[...] = jnp.zeros_like(d_send)
-        for i in range(PROJ):
-            first = (i % 7) * PROJ
-            d_send[i // 7, :, first : first + PROJ] = dmat_ref[i]
-        d_own[at_x * height + at_y] = d_send[...]
 
         @pl.when(jnp.logical_not(is_envoy))
         def _():
@@ -251,22 +249,19 @@
                 here.at[last_group], inc=1, device_id={"grid": envoy}, device_id_type=MESH
             )
 
-        def send1(count, carry):
-            step = peers - 1 - count
-            target = lax.rem(me + far(step), grid_count)
-            to_grid(msg1.at[target], got1.at[me], s1, r1.at[step // 16], target).start()
-            return carry
-
-        @pl.when(jnp.logical_not(is_envoy))
-        def _():
-            lax.fori_loop(0, peers, send1, 0, unroll=9)
-
-        @pl.when(is_envoy)
-        def _():
-            for group in range(groups):
-                sent = max(16 * group - 1, 0)
-                pl.semaphore_wait(here.at[groups - 1 - group], 16 * group + 15 - sent)
-                lax.fori_loop(sent, 16 * group + 15, send1, 0)
+        for group in reversed(range(groups)):
+
+            @pl.when(is_envoy)
+            def _(group=group):
+                pl.semaphore_wait(here.at[group], 16 if group < groups - 1 else 15)
+
+            for pair in reversed(range(8 * group, 8 * group + 8)):
+                for offset in reversed(far(pair)):
+                    if offset > 0:
+                        target = wrap(me + offset)
+                        to_grid(
+                            msg1.at[target], got1.at[me], s1, r1.at[group], target
+                        ).start()
 
         if band_count > 1:
 
@@ -286,9 +281,21 @@
         for copy in atom_copies:
             copy.start()
 
+        inputs[3].wait()
+        d_send[...] = jnp.zeros_like(d_send)
+        for i in range(PROJ):
+            first = (i % 7) * PROJ
+            d_send[i // 7, :, first : first + PROJ] = dmat_ref[i]
+        d_own[at_x * height + at_y] = d_send[0:2]
+        d_rest[chip] = d_send[2]
         for step in range(1, height):
             other = lax.rem(at_y + step, height) * width + at_x
-            to_grid(d_send, d_own.at[at_x * height + at_y], sd, rd, 2 * other + core).start()
+            to_grid(
+                d_send.at[pl.ds(0, 2)], d_own.at[at_x * height + at_y], sd, rd, 2 * other + core
+            ).start()
+        for step in range(1, width):
+            other = at_y * width + lax.rem(at_x + step, width)
+            to_grid(d_send.at[2], d_rest.at[chip], se, re, 2 * other + core).start()
 
         inputs[5].wait()
         for plane in range(PLANES):
@@ -309,10 +316,12 @@
         atoms = atom_ref[...]
         place = iota((half * ATOMS, PAIRS), 0)
         slot = place // ATOMS
-        atom_base = ((slot % height) * width + slot // height) * (2 * ATOMS) + place % ATOMS
         for which in range(2):
-            shift = jnp.where(which == 0, core, 1 - core) * ATOMS
-            d_pick[which] = jnp.where(atom_base + shift == atoms, 1.0, 0.0).astype(BF16)
+            shift = (core if which == 0 else 1 - core) * ATOMS + place % ATOMS
+            for order, holder in enumerate([(slot % height) * width + slot // height, slot]):
+                d_pick[which, order] = jnp.where(
+                    holder * (2 * ATOMS) + shift == atoms, 1.0, 0.0
+                ).astype(BF16)
         wide = jnp.concatenate([atom_col[...], atom_col[...]], axis=1)
         same[0] = jnp.where(wide == atom_row, 1.0, 0.0).astype(BF16)
         for i in range(4):
@@ -339,10 +348,7 @@
                 settle(got1.at[pl.ds(0, 16)], r1.at[group])
             total = jnp.zeros((BANDS * BOX, 2 * PLANES * BOX), F32)
             for pair in range(8):
-                senders = [
-                    lax.rem(me + grid_count - far(16 * group + 2 * pair + k), grid_count)
-                    for k in range(2)
-                ]
+                senders = [wrap(me + grid_count - offset) for offset in far(8 * group + pair)]
                 data = [got1[sender] for sender in senders]
                 codes = pltpu.roll(jnp.concatenate(data, axis=0), 0, 1, stride=16, stride_axis=0)
                 codes = jnp.where(code_place, codes, 0.0)
@@ -380,7 +386,6 @@
             def _():
                 tell_group()
 
-        lax.fori_loop(groups // 2, groups - 1, fill, 0)
         settle(d_own.at[pl.ds(0, height - 1)], rd)
 
         def column(offset):
@@ -394,8 +399,13 @@
         def to_mate(block):
             to_grid(d_own.at[block], d_mate.at[block], sm, rm, 2 * chip + 1 - core).start()
 
+        settle(d_rest.at[pl.ds(0, width - 1)], re)
+        line = d_rest.at[pl.ds(at_y * width, width)]
+        for step in range(1, height):
+            other = lax.rem(at_y + step, height) * width + at_x
+            to_grid(line, line, sg, rg, 2 * other + core).start()
         to_mate(column(0))
-        lax.fori_loop(groups - 1, groups, fill, 0)
+        lax.fori_loop(groups // 2, groups, fill, 0)
 
         box_hi, box_lo = halves(box_ref[...].T)
         turned = mm(box_hi, yt_ref[0]) + mm(box_lo, yt_ref[0]) + mm(box_hi, yt_ref[1])
@@ -470,17 +480,24 @@
         for i, offset in ((1, 1), (2, -1), (0, 2)):
             settle(d_own.at[pl.ds(0, height)], rx.at[i])
             to_mate(column(-offset))
-        for q in range(3):
-            d_hi, d_lo = halves(d_own[:, q].reshape(half * ATOMS, N))
-            slots = mm(d_hi, d_pick[0], TN) + mm(d_lo, d_pick[0], TN)
-            for lanes in range(2):
-                d_slot[lanes, q * N : (q + 1) * N, :] = slots[:, lanes * N : (lanes + 1) * N]
+        settle(d_rest.at[pl.ds(0, half - width)], rg)
+        rest_copy = to_grid(d_rest, rest_mate, sh, rh, 2 * chip + 1 - core)
+        rest_copy.start()
+        def gather_couplings(which, main, rest):
+            for q in range(3):
+                values = main[:, q] if q < 2 else rest[...]
+                d_hi, d_lo = halves(values.reshape(half * ATOMS, N))
+                pick = d_pick[which, q // 2]
+                slots = mm(d_hi, pick, TN) + mm(d_lo, pick, TN)
+                for lanes in range(2):
+                    part = slots[:, lanes * N : (lanes + 1) * N]
+                    rows = slice(q * N, (q + 1) * N)
+                    d_slot[lanes, rows, :] = part if which == 0 else d_slot[lanes, rows, :] + part
+
+        gather_couplings(0, d_own, d_rest)
         settle(d_mate, rm)
-        for q in range(3):
-            d_hi, d_lo = halves(d_mate[:, q].reshape(half * ATOMS, N))
-            slots = mm(d_hi, d_pick[1], TN) + mm(d_lo, d_pick[1], TN)
-            for lanes in range(2):
-                d_slot[lanes, q * N : (q + 1) * N, :] += slots[:, lanes * N : (lanes + 1) * N]
+        rest_copy.wait_recv()
+        gather_couplings(1, d_mate, rest_mate)
 
         if band_count > 1:
 
@@ -598,7 +615,11 @@
                     )
 
         def partners(step):
-            return [lax.rem(me + far(batch * step + k), grid_count) for k in range(batch)]
+            return [
+                wrap(me + offset)
+                for pair in range(batch // 2)
+                for offset in far(batch // 2 * step + pair)
+            ]
 
         def send2(target):
             to_grid(msg2.at[target], got2.at[me], s2, r2, target).start()
@@ -634,6 +655,9 @@
         settle(msg1.at[pl.ds(0, peers)], s1)
         settle(msg2.at[pl.ds(0, peers)], s2)
         settle(d_own.at[pl.ds(0, height - 1)], sd)
+        settle(d_rest.at[pl.ds(0, width - 1)], se)
+        settle(d_rest.at[pl.ds(0, half - width)], sg)
+        rest_copy.wait_send()
         for i in range(3):
             settle(d_own.at[pl.ds(0, height)], sx.at[i])
         settle(d_mate, sm)
@@ -715,8 +739,10 @@
                 pltpu.VMEM((4, 1, PAIRS), jnp.int32),
                 pltpu.VMEM((PAIRS, N), F32),
                 pltpu.VMEM((N, ROWS), F32),
-                pltpu.VMEM((half, 3, ATOMS, N), F32),
-                pltpu.VMEM((half, 3, ATOMS, N), F32),
+                pltpu.VMEM((half, 2, ATOMS, N), F32),
+                pltpu.VMEM((half, 2, ATOMS, N), F32),
+                pltpu.VMEM((half, ATOMS, N), F32),
+                pltpu.VMEM((half, ATOMS, N), F32),
                 pltpu.VMEM((2, 3 * N + 24, N), F32),
                 pltpu.VMEM((3, ATOMS, N), F32),
                 pltpu.VMEM((PROJ * COMBOS, PAIRS), F32),
@@ -728,10 +754,10 @@
                 pltpu.VMEM((ROWS, N), F32),
                 pltpu.VMEM((8, N), F32),
                 pltpu.VMEM((ROWS, PAIRS), BF16),
-                pltpu.VMEM((2, half * ATOMS, PAIRS), BF16),
+                pltpu.VMEM((2, 2, half * ATOMS, PAIRS), BF16),
                 pltpu.VMEM((5, PAIRS, PAIRS), BF16),
                 pltpu.SemaphoreType.REGULAR((grid_count // 16,)), pltpu.SemaphoreType.REGULAR,
-                dma((12,)), dma, dma, dma((grid_count // 16,)), dma, dma, dma, dma, dma((3,)), dma((3,)), dma, dma,
+                dma((12,)), dma, dma, dma((grid_count // 16,)), dma, dma, dma, dma, dma((3,)), dma((3,)), dma, dma, dma, dma, dma, dma, dma, dma,
                 dma((4,)), dma((4,)), dma((4, 3)), dma((4, 3)), dma, dma, dma, dma,
             ],
             compiler_params=pltpu.CompilerParams(

time: 46 us -> 44.4 us (0.965)
  the two profiles are of different devices: /device:TPU:9 before, /device:TPU:1 now
where the time goes in v6:
time: 44.4 us; the launch traced here: 44.3 us
  Pallas kernels  43.6 us (98%)
  between operations  0.64 us (1%)
    pallas_call x1, Pallas kernels, step(): pl.pallas_call(make_kernel(grid_count, band_count), out_shape=(jax.ShapeD...  41.6 us
    pallas_call x1, Pallas kernels, step(): pl.pallas_call(finish, out_shape=(jax.ShapeDtypeStruct(psi_g.shape, F32),...  2.01 us

profile of v6, /device:TPU:1, one launch (start us, length us, event | category | flops | bytes accessed | tf_op | source)
XLA Modules:
  0.0 44.3 jit_solution(14754013265951589336)
XLA Ops:
  0.6 41.6 %shard_map.140 = (f32[64,4,128]{2,1,0:T(4,128)}, f32[256,128]{1,0:T(8,128)}) custom-call(f32[2,2,48,128]{3,2,1,0:T(8,128)} %psi_ref.1, s32[1,48]{1,0:T(1,128)} %bitcast.9, bf16[2,256,256]{2,1,0:T(8,128)(2,1)} %constant.10.clone.xt_in.table_ref, f32[18,8,18]{2,1,0:T(8,128)} %bitcast.8, s32[1,256]{1,0:T(1,128)} %bitcast.11, f32[2,128,128]{2,1,0:T(8,128)} %vloc_in.1, ...), custom_call_target="tpu_custom_call" | custom-call | tf_op jit(solution)/shard_map/pallas_call | solution.py:706
  42.2 2.0 %shard_map.141 = (f32[2,2,48,128]{3,2,1,0:T(8,128)}, f32[256,128]{1,0:T(8,128)}) custom-call(f32[2,2,48,128]{3,2,1,0:T(8,128)} %psi_ref.1, s32[1,48]{1,0:T(1,128)} %bitcast.10, bf16[2,256,256]{2,1,0:T(8,128)(2,1)} %constant.10.clone.xt_in.table_ref, f32[64,4,128]{2,1,0:T(4,128)} %get-tuple-element.6.got_ref, f32[256,128]{1,0:T(8,128)} %get-tuple-element.7.dens_in), custom_call_target="tpu_custom_call" | custom-call | tf_op jit(solution)/shard_map/pallas_call | solution.py:781

commit v7 on v6

--- a/solution.py
+++ b/solution.py
@@ -127,7 +127,7 @@
             return half + pair, half - 1 - pair
 
         barrier = pltpu.get_barrier_semaphore()
-        envoy = 0
+        envoy = 2
         is_envoy = me == envoy
 
         apart = wrap(me - envoy + grid_count)
@@ -182,7 +182,7 @@
                     )
                     return carry
 
-                lax.fori_loop(1, grid_count, pass_on, 0)
+                lax.fori_loop(1, grid_count, pass_on, 0, unroll=9)
 
         def send_parts():
             @pl.when(jnp.logical_not(is_envoy))
@@ -249,6 +249,26 @@
                 here.at[last_group], inc=1, device_id={"grid": envoy}, device_id_type=MESH
             )
 
+        def prepare():
+            inputs[5].wait()
+            for plane in range(PLANES):
+                vloc_t[:, plane * N : (plane + 1) * N] = vloc_ref[plane].T
+            atom_row = atom_ref[...].astype(F32)
+            for part in range(2):
+                atom_col[part * N : (part + 1) * N, :] = jnp.broadcast_to(
+                    atom_row[:, part * N : (part + 1) * N], (N, N)
+                ).T
+            for copy in inputs[6:]:
+                copy.wait()
+            for i in range(PROJ):
+                for part in range(2):
+                    proj_t[i, :, part * N : (part + 1) * N] = proj_buf[i, part * N : (part + 1) * N, :].T
+
+        inputs[4].wait()
+        @pl.when(is_envoy)
+        def _():
+            prepare()
+
         for group in reversed(range(groups)):
 
             @pl.when(is_envoy)
@@ -274,7 +294,6 @@
                     )
 
         near = [lax.rem(me + off + grid_count, grid_count) for off in (1, -1, 2, -2)]
-        inputs[4].wait()
         atom_copies = [
             to_grid(atom_ref, near_atom.at[i], sa.at[i], ra.at[i], near[i]) for i in range(4)
         ]
@@ -297,20 +316,11 @@
             other = at_y * width + lax.rem(at_x + step, width)
             to_grid(d_send.at[2], d_rest.at[chip], se, re, 2 * other + core).start()
 
-        inputs[5].wait()
-        for plane in range(PLANES):
-            vloc_t[:, plane * N : (plane + 1) * N] = vloc_ref[plane].T
+        @pl.when(jnp.logical_not(is_envoy))
+        def _():
+            prepare()
+
         atom_row = atom_ref[...].astype(F32)
-        for part in range(2):
-            atom_col[part * N : (part + 1) * N, :] = jnp.broadcast_to(
-                atom_row[:, part * N : (part + 1) * N], (N, N)
-            ).T
-        for copy in inputs[6:]:
-            copy.wait()
-        for i in range(PROJ):
-            for part in range(2):
-                proj_t[i, :, part * N : (part + 1) * N] = proj_buf[i, part * N : (part + 1) * N, :].T
-
         local_row = row_ref[...] - me * ROWS
         row_pick[...] = jnp.where(iota((ROWS, PAIRS), 0) == local_row, 1.0, 0.0).astype(BF16)
         atoms = atom_ref[...]
@@ -324,9 +334,6 @@
                 ).astype(BF16)
         wide = jnp.concatenate([atom_col[...], atom_col[...]], axis=1)
         same[0] = jnp.where(wide == atom_row, 1.0, 0.0).astype(BF16)
-        for i in range(4):
-            atom_copies[i].wait_recv()
-            same[1 + i] = jnp.where(wide == near_atom[i].astype(F32), 1.0, 0.0).astype(BF16)
 
         box_ref[...] = jnp.zeros_like(box_ref)
         row_id = iota((BANDS * BOX, N), 0).astype(F32).astype(BF16)
@@ -344,7 +351,7 @@
             group = groups - 1 - step
             group = jnp.where(group > last_group, group, group - 1)
             group = jnp.where(step == groups - 1, last_group, group)
-            with jax.named_scope("s_fillwait"):
+            with jax.named_scope("columns_arrive"):
                 settle(got1.at[pl.ds(0, 16)], r1.at[group])
             total = jnp.zeros((BANDS * BOX, 2 * PLANES * BOX), F32)
             for pair in range(8):
@@ -407,6 +414,12 @@
         to_mate(column(0))
         lax.fori_loop(groups // 2, groups, fill, 0)
 
+        if band_count > 1:
+
+            @pl.when(early)
+            def _():
+                tell_group()
+
         box_hi, box_lo = halves(box_ref[...].T)
         turned = mm(box_hi, yt_ref[0]) + mm(box_lo, yt_ref[0]) + mm(box_hi, yt_ref[1])
         mid, end = PLANES * BOX, BANDS * N
@@ -434,10 +447,6 @@
 
         if band_count > 1:
 
-            @pl.when(early)
-            def _():
-                tell_group()
-
             @pl.when(jnp.logical_not(early))
             def _():
                 send_parts()
@@ -471,6 +480,9 @@
             for copy in coeff_copies[-1]:
                 copy.start()
 
+        for i in range(4):
+            atom_copies[i].wait_recv()
+            same[1 + i] = jnp.where(wide == near_atom[i].astype(F32), 1.0, 0.0).astype(BF16)
         if band_count > 1:
 
             @pl.when(early)
@@ -508,7 +520,7 @@
         c_hi, c_lo = halves(coeff[...])
         total = mm(c_hi, same[0], NT) + mm(c_lo, same[0], NT)
         for i in range(4):
-            with jax.named_scope("s_coefwait"):
+            with jax.named_scope("coefficients_arrive"):
                 for part in range(3):
                     coeff_copies[part][i].wait_recv()
             c_hi, c_lo = halves(near_coeff[i])
@@ -631,8 +643,16 @@
                 send2(target)
             return carry
 
-        lax.fori_loop(0, grid_count // batch - 1, take_and_send, 0)
-        targets = partners(grid_count // batch - 1)
+        batches = grid_count // batch
+        lax.fori_loop(0, batches // 2, take_and_send, 0)
+        if band_count > 1:
+
+            @pl.when(foremost)
+            def _():
+                add_parts()
+
+        lax.fori_loop(batches // 2, batches - 1, take_and_send, 0)
+        targets = partners(batches - 1)
         take(targets)
         for target in targets[:-1]:
             send2(target)
@@ -640,10 +660,6 @@
         own_back.start()
 
         if band_count > 1:
-
-            @pl.when(foremost)
-            def _():
-                add_parts()
 
             settle(dens_full.at[pl.ds(0, ROWS - share)], rf)
         dens_out = pltpu.make_async_copy(dens_full, dens_hbm, in_sem.at[0])

time: 44.4 us -> 42.6 us (0.959)
  Pallas kernels: 43.6 us -> 41.8 us
    pallas_call x1, Pallas kernels: 41.6 us -> 39.8 us  [step(): pl.pallas_call(make_kernel(grid_count, band_count), out_shape=(jax.ShapeD...]
where the time goes in v7:
time: 42.6 us; the launch traced here: 42.4 us
  Pallas kernels  41.8 us (98%)
  between operations  0.64 us (2%)
    pallas_call x1, Pallas kernels, step(): pl.pallas_call(make_kernel(grid_count, band_count), out_shape=(jax.ShapeD...  39.8 us
    pallas_call x1, Pallas kernels, step(): pl.pallas_call(finish, out_shape=(jax.ShapeDtypeStruct(psi_g.shape, F32),...  2.01 us

profile of v7, /device:TPU:1, one launch (start us, length us, event | category | flops | bytes accessed | tf_op | source)
XLA Modules:
  0.0 42.4 jit_solution(16863230299162336119)
XLA Ops:
  0.6 39.8 %shard_map.140 = (f32[64,4,128]{2,1,0:T(4,128)}, f32[256,128]{1,0:T(8,128)}) custom-call(f32[2,2,48,128]{3,2,1,0:T(8,128)} %psi_ref.1, s32[1,48]{1,0:T(1,128)} %bitcast.9, bf16[2,256,256]{2,1,0:T(8,128)(2,1)} %constant.10.clone.xt_in.table_ref, f32[18,8,18]{2,1,0:T(8,128)} %bitcast.8, s32[1,256]{1,0:T(1,128)} %bitcast.11, f32[2,128,128]{2,1,0:T(8,128)} %vloc_in.1, ...), custom_call_target="tpu_custom_call" | custom-call | tf_op jit(solution)/shard_map/pallas_call | solution.py:722
  40.4 2.0 %shard_map.141 = (f32[2,2,48,128]{3,2,1,0:T(8,128)}, f32[256,128]{1,0:T(8,128)}) custom-call(f32[2,2,48,128]{3,2,1,0:T(8,128)} %psi_ref.1, s32[1,48]{1,0:T(1,128)} %bitcast.10, bf16[2,256,256]{2,1,0:T(8,128)(2,1)} %constant.10.clone.xt_in.table_ref, f32[64,4,128]{2,1,0:T(4,128)} %get-tuple-element.6.got_ref, f32[256,128]{1,0:T(8,128)} %get-tuple-element.7.dens_in), custom_call_target="tpu_custom_call" | custom-call | tf_op jit(solution)/shard_map/pallas_call | solution.py:797

commit v8 on v7

--- a/solution.py
+++ b/solution.py
@@ -393,6 +393,7 @@
             def _():
                 tell_group()
 
+        lax.fori_loop(groups // 2, groups - 1, fill, 0)
         settle(d_own.at[pl.ds(0, height - 1)], rd)
 
         def column(offset):
@@ -412,7 +413,7 @@
             other = lax.rem(at_y + step, height) * width + at_x
             to_grid(line, line, sg, rg, 2 * other + core).start()
         to_mate(column(0))
-        lax.fori_loop(groups // 2, groups, fill, 0)
+        lax.fori_loop(groups - 1, groups, fill, 0)
 
         if band_count > 1:
 

time: 42.6 us -> 43.2 us (1.014)
  Pallas kernels: 41.8 us -> 42.4 us
    pallas_call x1, Pallas kernels: 39.8 us -> 40.4 us  [step(): pl.pallas_call(make_kernel(grid_count, band_count), out_shape=(jax.ShapeD...]
where the time goes in v8:
time: 43.2 us; the launch traced here: 43 us
  Pallas kernels  42.4 us (98%)
  between operations  0.64 us (1%)
    pallas_call x1, Pallas kernels, step(): pl.pallas_call(make_kernel(grid_count, band_count), out_shape=(jax.ShapeD...  40.4 us
    pallas_call x1, Pallas kernels, step(): pl.pallas_call(finish, out_shape=(jax.ShapeDtypeStruct(psi_g.shape, F32),...  2.01 us

profile of v8, /device:TPU:1, one launch (start us, length us, event | category | flops | bytes accessed | tf_op | source)
XLA Modules:
  0.0 43.0 jit_solution(9863919576465301819)
XLA Ops:
  0.6 40.4 %shard_map.140 = (f32[64,4,128]{2,1,0:T(4,128)}, f32[256,128]{1,0:T(8,128)}) custom-call(f32[2,2,48,128]{3,2,1,0:T(8,128)} %psi_ref.1, s32[1,48]{1,0:T(1,128)} %bitcast.9, bf16[2,256,256]{2,1,0:T(8,128)(2,1)} %constant.10.clone.xt_in.table_ref, f32[18,8,18]{2,1,0:T(8,128)} %bitcast.8, s32[1,256]{1,0:T(1,128)} %bitcast.11, f32[2,128,128]{2,1,0:T(8,128)} %vloc_in.1, ...), custom_call_target="tpu_custom_call" | custom-call | tf_op jit(solution)/shard_map/pallas_call | solution.py:723
  41.0 2.0 %shard_map.141 = (f32[2,2,48,128]{3,2,1,0:T(8,128)}, f32[256,128]{1,0:T(8,128)}) custom-call(f32[2,2,48,128]{3,2,1,0:T(8,128)} %psi_ref.1, s32[1,48]{1,0:T(1,128)} %bitcast.10, bf16[2,256,256]{2,1,0:T(8,128)(2,1)} %constant.10.clone.xt_in.table_ref, f32[64,4,128]{2,1,0:T(4,128)} %get-tuple-element.6.got_ref, f32[256,128]{1,0:T(8,128)} %get-tuple-element.7.dens_in), custom_call_target="tpu_custom_call" | custom-call | tf_op jit(solution)/shard_map/pallas_call | solution.py:798
